TPU v7x, 32 devices: a whole 2x2x4 slice. The times are simulated.
32 devices in a mesh: pair: 4 (over x, core), virt: 8 (over z, y).
Axes of the slice: x: 2, y: 2, z: 4, core: 2. Of those that a mesh axis runs over, the one named last changes fastest.
Arguments:
- amplitudes: bfloat16 [1024, 256], P(('pair', 'virt')), may hold values from -6 to 6
- integrals: bfloat16 [256, 16384], P('pair', 'virt'), may hold values from -0.375 to 0.375
- amp_mask: int32 [16, 4], P('pair'), may hold values from 0 to 1, as said below
- integral_mask: int32 [4, 256], P('pair', 'virt'), may hold values 0 or 1
Outputs:
- ladder: bfloat16 [1024, 16384], P('pair', 'virt')
Inputs may be any that keep to these rules, and one draw needn't show every extreme that they name: `amp_mask`: 0 or 1. For every block of 4 consecutive ij tiles, the cd tiles that hold nonzeros lie within one cyclic window of cd tiles common to the block, whose length may differ from block to block.
All inputs are finite; a program needn't handle non-finite values. No bound on the sum of `integral_mask` on one device may be relied on, other than what follows from the above.
Results may differ from a plain program's by a relative error of at most 0.001.
Values may be sent and summed in bfloat16 or wider, within the bound.
A program may use at most 64 MiB of HBM per device.

v0:
```python
import jax
import jax.numpy as jnp
from jax import lax
from jax.sharding import PartitionSpec as P

TILE = 64


def widened_mask(values, mask):
    tile_rows, tile_columns = mask.shape
    shaped = values.reshape(tile_rows, TILE, tile_columns, TILE)
    return (shaped * mask.astype(values.dtype)[:, None, :, None]).reshape(values.shape)


def on_device(amplitudes, integrals, amp_mask, integral_mask):
    full_amp = lax.all_gather(amplitudes, "virt", axis=0, tiled=True)
    masked_amp = widened_mask(full_amp, amp_mask)
    own_panel = widened_mask(integrals, integral_mask)
    whole_panel = lax.all_gather(own_panel, "pair", axis=0, tiled=True)
    result = jnp.dot(masked_amp, whole_panel, preferred_element_type=jnp.float32)
    return result.astype(jnp.bfloat16)


def solution(mesh):
    in_specs = (P(("pair", "virt"), None), P("pair", "virt"), P("pair", None), P("pair", "virt"))
    out_specs = P("pair", "virt")
    return jax.shard_map(
        on_device, mesh=mesh, in_specs=in_specs, out_specs=out_specs, check_vma=False
    )
```

profile of v0, /device:TPU:0, one launch (start us, length us, event | category | flops | bytes accessed | tf_op | source)
XLA Modules:
  0.0 51.9 jit_solution(7016548213648039129)
XLA Ops:
  6.5 0.0 copy-start
  6.5 0.0 all-gather.2.cloned.1.call-start
  6.5 0.7 %convert_bitcast_fusion = bf16[32]{0:T(256)(128)(2,1)S(1)} fusion(s32[1,32]{1,0:T(1,128)} %param.7), kind=kLoop, calls=%fused_computation.3 | loop fusion | flops 32 | bytes 192 | tf_op jit(solution)/shard_map/mul | solution.py:12
  7.2 0.1 mul.32
  7.3 0.1 mul.33
  7.4 1.7 %broadcast_multiply_fusion = bf16[64,2048]{1,0:T(8,128)(2,1)} fusion(bf16[64,2048]{1,0:T(8,128)(2,1)} %param.5, bf16[2048]{0:T(1024)(128)(2,1)S(1)} %mul.33), kind=kLoop, calls=%fused_computation.1 | loop fusion | flops 131072 | bytes 528384 | tf_op jit(solution)/shard_map/mul | solution.py:12
  9.0 0.0 all-gather.2.cloned.1.call-update
  9.1 0.7 %convert_element_type.9 = bf16[4,4]{1,0:T(4,128)(2,1)S(1)} convert(s32[4,4]{1,0:T(4,128)} %param.6) | non-fusion elementwise | flops 16 | bytes 96 | tf_op jit(solution)/shard_map/convert_element_type | solution.py:12
  9.8 0.1 mul.28
  9.9 0.2 mul.29
  10.1 0.0 copy-done
  10.1 32.3 %all_gather.6 = bf16[256,256]{1,0:T(8,128)(2,1)S(1)} all-gather(bf16[32,256]{1,0:T(8,128)(2,1)S(1)} %copy-done), channel_id=1, replica_groups=mesh['pair'=4,'virt'=8] {'virt'}, dimensions={0}, use_global_device_ids=true | all-gather | bytes 147456 | tf_op jit(solution)/shard_map/all_gather | solution.py:16
  42.4 0.0 all-gather.2.cloned.1.call-done
  42.4 2.6 %convolution_convert_fusion = bf16[256,2048]{1,0:T(8,128)(2,1)} fusion(bf16[256,2048]{1,0:T(8,128)(2,1)} %all-gather.2.cloned.1.call-done, bf16[256,256]{1,0:T(8,128)(2,1)S(1)} %all_gather.6, bf16[256,256]{1,0:T(8,128)(2,1)S(1)} %mul.29), kind=kOutput, calls=%fused_computation | convolution fusion | flops 269025280 | bytes 2359296 | tf_op jit(solution)/shard_map/dot_general | solution.py:20
Async XLA Ops:
  6.5 3.6 %copy-start = (bf16[32,256]{1,0:T(8,128)(2,1)S(1)}, bf16[32,256]{1,0:T(8,128)(2,1)}, u32[]{:S(2)}) copy-start(bf16[32,256]{1,0:T(8,128)(2,1)} %param.4) | copy-start | bytes 49156
  6.5 35.9 %all-gather.2.cloned.1.call-start = ((), (), s32[]{:S(2)}) async-start(), calls=%async_computation | async-start | bytes 1310720 | tf_op jit(solution)/shard_map/all_gather | solution.py:19
Sparse Core Ops, SparseCore 0:
  9.2 19.4 all-gather.1
where the time goes:
time: 52.2 us; the launch traced here: 51.9 us
  blocking collectives  32.3 us (62%)
  between operations  13.4 us (26%)
  other arithmetic  3.03 us (6%)
  matrix products  2.64 us (5%)
    all_gather x1, blocking collectives, on_device(): full_amp = lax.all_gather(amplitudes, 'virt', axis=0, tiled=True)  32.3 us
    dot_general x1, matrix products, on_device(): jnp.dot(masked_amp, whole_panel, preferred_element_type=jnp.float32)  2.64 us
    mul x2, other arithmetic, widened_mask(): shaped * mask.astype(values.dtype)[:, None, :, None]  2.34 us
  transfers between devices with their start and end apart: 1, of which 0 were waited for; matrix products, arithmetic and copies ran while one was open for 2% of the time, Pallas kernels for 0%

commit v1 on v0

v1 whole, which is shorter than its diff:
```python
import functools

import jax
import jax.numpy as jnp
from jax import lax
from jax.experimental import pallas as pl
from jax.experimental.pallas import tpu as pltpu
from jax.sharding import PartitionSpec as P

MESH = pl.DeviceIdType.MESH
CHUNK = 256
CORES = 2
F32 = jnp.float32
BF16 = jnp.bfloat16


def spread(tiles, length, axis):
    shape = (length, tiles) if axis == 0 else (tiles, length)
    place = lax.broadcasted_iota(jnp.int32, shape, axis)
    tile = lax.broadcasted_iota(jnp.int32, shape, 1 - axis)
    size = length // tiles
    inside = (place >= tile * size) & (place < (tile + 1) * size)
    return jnp.where(inside, 1.0, 0.0).astype(BF16)


def kernel(n_pair, n_virt, amp_hbm, int_hbm, amp_mask, int_mask, out,
           own, panel, amps, masked, local_sem, x_send, x_recv, f_send, f_recv, a_send, a_recv):
    me_p, me_v = lax.axis_index("pair"), lax.axis_index("virt")
    n_hi = n_pair // CORES
    hi, core = me_p // CORES, me_p % CORES
    partner = hi * CORES + (1 - core)
    depth, columns = int_hbm.shape
    rows = amp_hbm.shape[0]
    chunks = panel.shape[0]

    load = pltpu.make_async_copy(int_hbm, own, local_sem.at[0])
    load.start()
    barrier = pltpu.get_barrier_semaphore()

    def hi_peer(step):
        return ((hi + step) % n_hi) * CORES + core

    def greet(pair, virt):
        pl.semaphore_signal(barrier, inc=1, device_id=(pair, virt), device_id_type=MESH)

    for step in range(1, n_virt):
        greet(me_p, (me_v + step) % n_virt)
    for step in range(1, n_hi):
        greet(hi_peer(step), me_v)
    greet(partner, me_v)

    my_amps = amps.at[pl.ds(pl.multiple_of(me_v * rows, rows), rows)]
    keep = pltpu.make_async_copy(amp_hbm, my_amps, local_sem.at[1])
    keep.start()

    def block(pair, chunk):
        return panel.at[chunk, pl.ds(pl.multiple_of(pair * depth, depth), depth)]

    tiles = int_mask.shape[1]
    mask = jnp.broadcast_to(int_mask[...].astype(F32), (8, tiles)).astype(BF16)
    wide = jnp.dot(mask, spread(tiles, columns, 1), preferred_element_type=F32)[:1].astype(BF16)
    load.wait()
    for c in range(chunks):
        at = slice(c * CHUNK, (c + 1) * CHUNK)
        block(me_p, c)[...] = own[:, at] * wide[:, at]

    pl.semaphore_wait(barrier, n_virt - 1 + n_hi)

    def to_hi(step, c):
        mine = block(me_p, c)
        return pltpu.make_async_remote_copy(
            src_ref=mine, dst_ref=mine, send_sem=x_send.at[step, c], recv_sem=x_recv.at[step, c],
            device_id=(hi_peer(step), me_v), device_id_type=MESH)

    def to_partner(step, c):
        held = block(((hi - step + n_hi) % n_hi) * CORES + core, c)
        return pltpu.make_async_remote_copy(
            src_ref=held, dst_ref=held, send_sem=f_send.at[step, c], recv_sem=f_recv.at[step, c],
            device_id=(partner, me_v), device_id_type=MESH)

    def to_virt(step):
        return pltpu.make_async_remote_copy(
            src_ref=amp_hbm, dst_ref=my_amps, send_sem=a_send.at[step], recv_sem=a_recv.at[step],
            device_id=(me_p, (me_v + step) % n_virt), device_id_type=MESH)

    for c in range(chunks):
        for step in range(1, n_hi):
            to_hi(step, c).start()
    for step in range(1, n_virt):
        to_virt(step).start()
    for c in range(chunks):
        to_partner(0, c).start()

    row_tiles, col_tiles = amp_mask.shape
    all_rows, depths = amps.shape
    tall = jnp.dot(spread(row_tiles, all_rows, 0), amp_mask[...].astype(F32).astype(BF16),
                   preferred_element_type=F32).astype(BF16)
    full = jnp.dot(tall, spread(col_tiles, depths, 1), preferred_element_type=F32).astype(BF16)
    keep.wait()
    for step in range(1, n_virt):
        to_virt(step).wait_recv()
    masked[...] = amps[...] * full

    def multiply(c):
        for step in range(n_hi):
            to_partner(step, c).wait_recv()
        part = min(all_rows, 256)

        def some_rows(r):
            at = pl.ds(r * part, part)
            total = jnp.dot(masked[at, :], panel[c], preferred_element_type=F32)
            out[at, c * CHUNK:(c + 1) * CHUNK] = total.astype(BF16)

        if all_rows == part:
            some_rows(0)
        else:
            def body(r, carry):
                some_rows(r)
                return carry
            lax.fori_loop(0, all_rows // part, body, 0)

    for c in range(chunks):
        for step in range(1, n_hi):
            to_hi(step, c).wait_recv()
            to_partner(step, c).start()
        if c:
            multiply(c - 1)
    multiply(chunks - 1)

    for step in range(1, n_virt):
        to_virt(step).wait_send()
    for c in range(chunks):
        for step in range(1, n_hi):
            to_hi(step, c).wait_send()
        for step in range(n_hi):
            to_partner(step, c).wait_send()


def solution(mesh):
    n_pair, n_virt = mesh.shape["pair"], mesh.shape["virt"]
    n_hi = n_pair // CORES

    def on_device(amplitudes, integrals, amp_mask, integral_mask):
        rows, depths = amplitudes.shape
        depth, columns = integrals.shape
        chunks = columns // CHUNK
        dma = pltpu.SemaphoreType.DMA
        vmem = pl.BlockSpec(memory_space=pltpu.VMEM)
        anywhere = pl.BlockSpec(memory_space=pl.ANY)
        return pl.pallas_call(
            functools.partial(kernel, n_pair, n_virt),
            out_shape=jax.ShapeDtypeStruct((rows * n_virt, columns), BF16),
            in_specs=[anywhere, anywhere, vmem, vmem],
            out_specs=vmem,
            scratch_shapes=[
                pltpu.VMEM((depth, columns), BF16),
                pltpu.VMEM((chunks, depths, CHUNK), BF16),
                pltpu.VMEM((rows * n_virt, depths), BF16),
                pltpu.VMEM((rows * n_virt, depths), BF16),
                dma((2,)),
                dma((n_hi, chunks)), dma((n_hi, chunks)),
                dma((n_hi, chunks)), dma((n_hi, chunks)),
                dma((n_virt,)), dma((n_virt,)),
            ],
            compiler_params=pltpu.CompilerParams(
                collective_id=0, has_side_effects=True, vmem_limit_bytes=32 * 2 ** 20),
        )(amplitudes, integrals, amp_mask, integral_mask)

    in_specs = (P(("pair", "virt"), None), P("pair", "virt"), P("pair", None), P("pair", "virt"))
    return jax.shard_map(
        on_device, mesh=mesh, in_specs=in_specs, out_specs=P("pair", "virt"), check_vma=False
    )
```

time: 52.2 us -> 20.2 us (0.39)
  blocking collectives: 32.3 us -> 0 us
  Pallas kernels: 0 us -> 15.9 us
  between operations: 13.4 us -> 0.01 us
  local copies, waits for them, and re-layouts: 0.52 us -> 3.97 us
  other arithmetic: 3.03 us -> 0 us
  matrix products: 2.64 us -> 0 us
    all_gather x1 -> x0, blocking collectives: 32.3 us -> none  [on_device(): full_amp = lax.all_gather(amplitudes, 'virt', axis=0, tiled=True)]
    pallas_call x0 -> x1, Pallas kernels: none -> 15.9 us  [on_device(): pl.pallas_call(functools.partial(kernel, n_pair, n_virt), out_shape=jax.S...]
    unnamed x2 -> x9, local copies, waits for them, and re-layouts: 0.01 us -> 3.97 us
    dot_general x1 -> x0, matrix products: 2.64 us -> none  [on_device(): jnp.dot(masked_amp, whole_panel, preferred_element_type=jnp.float32)]
    mul x2 -> x0, other arithmetic: 2.34 us -> none  [widened_mask(): shaped * mask.astype(values.dtype)[:, None, :, None]]
    convert_element_type x1 -> x0, other arithmetic: 0.69 us -> none  [widened_mask(): mask.astype(values.dtype)[:, None, :, None]]
  transfers between devices with their start and end apart: 1 -> 0, of which waited for: 0 -> 0; matrix products, arithmetic and copies ran while one was open for 2% -> 0% of each run, Pallas kernels for 0% -> 0%
where the time goes in v1:
time: 20.2 us; the launch traced here: 19.9 us
  Pallas kernels  15.9 us (79%)
  local copies, waits for them, and re-layouts  3.97 us (20%)
    pallas_call x1, Pallas kernels, on_device(): pl.pallas_call(functools.partial(kernel, n_pair, n_virt), out_shape=jax.S...  15.9 us
    unnamed x9, local copies, waits for them, and re-layouts  3.97 us

profile of v1, /device:TPU:0, one launch (start us, length us, event | category | flops | bytes accessed | tf_op | source)
XLA Modules:
  0.0 19.9 jit_solution(12944260469246865712)
XLA Ops:
  0.0 0.0 copy-start
  0.0 0.9 %copy-done = bf16[64,2048]{1,0:T(8,128)(2,1)S(1)} copy-done((bf16[64,2048]{1,0:T(8,128)(2,1)S(1)}, bf16[64,2048]{1,0:T(8,128)(2,1)}, u32[]{:S(2)}) %copy-start) | copy-done | bytes 262168
  1.0 0.0 copy-start.1
  1.0 0.7 %copy-done.1 = bf16[32,256]{1,0:T(8,128)(2,1)S(1)} copy-done((bf16[32,256]{1,0:T(8,128)(2,1)S(1)}, bf16[32,256]{1,0:T(8,128)(2,1)}, u32[]{:S(2)}) %copy-start.1) | copy-done | bytes 16408
  1.7 0.0 copy-start.2
  1.7 0.7 %copy-done.2 = s32[4,4]{1,0:T(4,128)S(1)} copy-done((s32[4,4]{1,0:T(4,128)S(1)}, s32[4,4]{1,0:T(4,128)}, u32[]{:S(2)}) %copy-start.2) | copy-done | bytes 88
  2.4 0.0 copy-start.3
  2.4 0.7 %copy-done.3 = s32[1,32]{1,0:T(1,128)S(1)} copy-done((s32[1,32]{1,0:T(1,128)S(1)}, s32[1,32]{1,0:T(1,128)}, u32[]{:S(2)}) %copy-start.3) | copy-done | bytes 152
  3.0 15.9 %shard_map.46 = bf16[256,2048]{1,0:T(8,128)(2,1)S(1)} custom-call(bf16[32,256]{1,0:T(8,128)(2,1)S(1)} %copy-done.1, bf16[64,2048]{1,0:T(8,128)(2,1)S(1)} %copy-done, s32[4,4]{1,0:T(4,128)S(1)} %copy-done.2, s32[1,32]{1,0:T(1,128)S(1)} %copy-done.3), custom_call_target="tpu_custom_call" | custom-call | tf_op jit(solution)/shard_map/pallas_call | solution.py:150
  19.0 1.0 %copy.6 = bf16[256,2048]{1,0:T(8,128)(2,1)} copy(bf16[256,2048]{1,0:T(8,128)(2,1)S(1)} %shard_map.46) | data formatting | bytes 2097152
Async XLA Ops:
  0.0 0.9 %copy-start = (bf16[64,2048]{1,0:T(8,128)(2,1)S(1)}, bf16[64,2048]{1,0:T(8,128)(2,1)}, u32[]{:S(2)}) copy-start(bf16[64,2048]{1,0:T(8,128)(2,1)} %int_hbm.1) | copy-start | bytes 786436
  1.0 0.7 %copy-start.1 = (bf16[32,256]{1,0:T(8,128)(2,1)S(1)}, bf16[32,256]{1,0:T(8,128)(2,1)}, u32[]{:S(2)}) copy-start(bf16[32,256]{1,0:T(8,128)(2,1)} %amp_hbm.1) | copy-start | bytes 49156
  1.7 0.7 %copy-start.2 = (s32[4,4]{1,0:T(4,128)S(1)}, s32[4,4]{1,0:T(4,128)}, u32[]{:S(2)}) copy-start(s32[4,4]{1,0:T(4,128)} %amp_mask.1) | copy-start | bytes 196
  2.4 0.7 %copy-start.3 = (s32[1,32]{1,0:T(1,128)S(1)}, s32[1,32]{1,0:T(1,128)}, u32[]{:S(2)}) copy-start(s32[1,32]{1,0:T(1,128)} %int_mask.1) | copy-start | bytes 388

commit v2 on v1

--- a/solution.py
+++ b/solution.py
@@ -23,8 +23,9 @@
     return jnp.where(inside, 1.0, 0.0).astype(BF16)
 
 
-def kernel(n_pair, n_virt, amp_hbm, int_hbm, amp_mask, int_mask, out,
-           own, panel, amps, masked, local_sem, x_send, x_recv, f_send, f_recv, a_send, a_recv):
+def kernel(n_pair, n_virt, amp_hbm, int_hbm, amp_mask_hbm, int_mask_hbm, out,
+           own, panel, amps, masked, amp_mask, int_mask, result,
+           local_sem, out_sem, x_send, x_recv, f_send, f_recv, a_send, a_recv):
     me_p, me_v = lax.axis_index("pair"), lax.axis_index("virt")
     n_hi = n_pair // CORES
     hi, core = me_p // CORES, me_p % CORES
@@ -35,6 +36,10 @@
 
     load = pltpu.make_async_copy(int_hbm, own, local_sem.at[0])
     load.start()
+    load_int_mask = pltpu.make_async_copy(int_mask_hbm, int_mask, local_sem.at[2])
+    load_int_mask.start()
+    load_amp_mask = pltpu.make_async_copy(amp_mask_hbm, amp_mask, local_sem.at[3])
+    load_amp_mask.start()
     barrier = pltpu.get_barrier_semaphore()
 
     def hi_peer(step):
@@ -57,8 +62,10 @@
         return panel.at[chunk, pl.ds(pl.multiple_of(pair * depth, depth), depth)]
 
     tiles = int_mask.shape[1]
+    repeat = spread(tiles, columns, 1)
+    load_int_mask.wait()
     mask = jnp.broadcast_to(int_mask[...].astype(F32), (8, tiles)).astype(BF16)
-    wide = jnp.dot(mask, spread(tiles, columns, 1), preferred_element_type=F32)[:1].astype(BF16)
+    wide = jnp.dot(mask, repeat, preferred_element_type=F32)[:1].astype(BF16)
     load.wait()
     for c in range(chunks):
         at = slice(c * CHUNK, (c + 1) * CHUNK)
@@ -83,23 +90,28 @@
             src_ref=amp_hbm, dst_ref=my_amps, send_sem=a_send.at[step], recv_sem=a_recv.at[step],
             device_id=(me_p, (me_v + step) % n_virt), device_id_type=MESH)
 
+    for step in range(1, n_virt):
+        to_virt(step).start()
     for c in range(chunks):
         for step in range(1, n_hi):
             to_hi(step, c).start()
-    for step in range(1, n_virt):
-        to_virt(step).start()
-    for c in range(chunks):
         to_partner(0, c).start()
 
     row_tiles, col_tiles = amp_mask.shape
     all_rows, depths = amps.shape
+    load_amp_mask.wait()
     tall = jnp.dot(spread(row_tiles, all_rows, 0), amp_mask[...].astype(F32).astype(BF16),
                    preferred_element_type=F32).astype(BF16)
-    full = jnp.dot(tall, spread(col_tiles, depths, 1), preferred_element_type=F32).astype(BF16)
-    keep.wait()
-    for step in range(1, n_virt):
-        to_virt(step).wait_recv()
-    masked[...] = amps[...] * full
+    masked[...] = jnp.dot(tall, spread(col_tiles, depths, 1), preferred_element_type=F32).astype(BF16)
+
+    def gather_amps():
+        keep.wait()
+        for step in range(1, n_virt):
+            to_virt(step).wait_recv()
+        masked[...] = amps[...] * masked[...]
+
+    def store(c):
+        return pltpu.make_async_copy(result.at[c], out.at[:, pl.ds(c * CHUNK, CHUNK)], out_sem.at[c])
 
     def multiply(c):
         for step in range(n_hi):
@@ -109,7 +121,7 @@
         def some_rows(r):
             at = pl.ds(r * part, part)
             total = jnp.dot(masked[at, :], panel[c], preferred_element_type=F32)
-            out[at, c * CHUNK:(c + 1) * CHUNK] = total.astype(BF16)
+            result[c, at, :] = total.astype(BF16)
 
         if all_rows == part:
             some_rows(0)
@@ -118,13 +130,18 @@
                 some_rows(r)
                 return carry
             lax.fori_loop(0, all_rows // part, body, 0)
+        store(c).start()
 
+    late = chunks // 2
     for c in range(chunks):
         for step in range(1, n_hi):
             to_hi(step, c).wait_recv()
             to_partner(step, c).start()
-        if c:
-            multiply(c - 1)
+        if c == late:
+            gather_amps()
+        if c >= late:
+            for ready in range(0 if c == late else c - 1, c):
+                multiply(ready)
     multiply(chunks - 1)
 
     for step in range(1, n_virt):
@@ -134,6 +151,7 @@
             to_hi(step, c).wait_send()
         for step in range(n_hi):
             to_partner(step, c).wait_send()
+        store(c).wait()
 
 
 def solution(mesh):
@@ -145,25 +163,28 @@
         depth, columns = integrals.shape
         chunks = columns // CHUNK
         dma = pltpu.SemaphoreType.DMA
-        vmem = pl.BlockSpec(memory_space=pltpu.VMEM)
-        anywhere = pl.BlockSpec(memory_space=pl.ANY)
+        hbm = pl.BlockSpec(memory_space=pltpu.HBM)
         return pl.pallas_call(
             functools.partial(kernel, n_pair, n_virt),
             out_shape=jax.ShapeDtypeStruct((rows * n_virt, columns), BF16),
-            in_specs=[anywhere, anywhere, vmem, vmem],
-            out_specs=vmem,
+            in_specs=[hbm] * 4,
+            out_specs=hbm,
             scratch_shapes=[
                 pltpu.VMEM((depth, columns), BF16),
                 pltpu.VMEM((chunks, depths, CHUNK), BF16),
                 pltpu.VMEM((rows * n_virt, depths), BF16),
                 pltpu.VMEM((rows * n_virt, depths), BF16),
-                dma((2,)),
+                pltpu.VMEM(amp_mask.shape, jnp.int32),
+                pltpu.VMEM(integral_mask.shape, jnp.int32),
+                pltpu.VMEM((chunks, rows * n_virt, CHUNK), BF16),
+                dma((4,)),
+                dma((chunks,)),
                 dma((n_hi, chunks)), dma((n_hi, chunks)),
                 dma((n_hi, chunks)), dma((n_hi, chunks)),
                 dma((n_virt,)), dma((n_virt,)),
             ],
             compiler_params=pltpu.CompilerParams(
-                collective_id=0, has_side_effects=True, vmem_limit_bytes=32 * 2 ** 20),
+                collective_id=0, has_side_effects=True, vmem_limit_bytes=60 * 2 ** 20),
         )(amplitudes, integrals, amp_mask, integral_mask)
 
     in_specs = (P(("pair", "virt"), None), P("pair", "virt"), P("pair", None), P("pair", "virt"))

time: 20.2 us -> 19.7 us (0.975)
  local copies, waits for them, and re-layouts: 3.97 us -> 2.3 us
  Pallas kernels: 15.9 us -> 17.2 us
    unnamed x9 -> x1, local copies, waits for them, and re-layouts: 3.97 us -> 2.3 us
    pallas_call x1, Pallas kernels: 15.9 us -> 17.2 us  [on_device(): pl.pallas_call(functools.partial(kernel, n_pair, n_virt), out_shape=jax.S...]
where the time goes in v2:
time: 19.7 us; the launch traced here: 19.5 us
  Pallas kernels  17.2 us (87%)
  local copies, waits for them, and re-layouts  2.3 us (12%)
    pallas_call x1, Pallas kernels, on_device(): pl.pallas_call(functools.partial(kernel, n_pair, n_virt), out_shape=jax.S...  17.2 us
    unnamed x1, local copies, waits for them, and re-layouts  2.3 us

profile of v2, /device:TPU:0, one launch (start us, length us, event | category | flops | bytes accessed | tf_op | source)
XLA Modules:
  0.0 19.5 jit_solution(15205482609883404696)
XLA Ops:
  0.0 17.2 %shard_map.46 = bf16[256,2048]{1,0:T(8,128)(2,1)} custom-call(bf16[32,256]{1,0:T(8,128)(2,1)} %amp_hbm.1, bf16[64,2048]{1,0:T(8,128)(2,1)} %int_hbm.1, s32[4,4]{1,0:T(4,128)} %amp_mask_hbm.1, s32[1,32]{1,0:T(1,128)} %int_mask_hbm.1), custom_call_target="tpu_custom_call" | custom-call | tf_op jit(solution)/shard_map/pallas_call | solution.py:167
  17.2 2.3 %copy.6 = bf16[256,2048]{1,0:T(8,128)(2,1)} copy(bf16[256,2048]{1,0:T(8,128)(2,1)} %shard_map.46) | data formatting | bytes 2097152

commit v3 on v2

--- a/solution.py
+++ b/solution.py
@@ -45,11 +45,17 @@
     def hi_peer(step):
         return ((hi + step) % n_hi) * CORES + core
 
+    rounds = n_virt.bit_length() - 1
+
+    def virt_peer(turn):
+        bit = 2 ** turn
+        return me_v + bit * (1 - 2 * ((me_v // bit) % 2))
+
     def greet(pair, virt):
         pl.semaphore_signal(barrier, inc=1, device_id=(pair, virt), device_id_type=MESH)
 
-    for step in range(1, n_virt):
-        greet(me_p, (me_v + step) % n_virt)
+    for turn in range(rounds):
+        greet(me_p, virt_peer(turn))
     for step in range(1, n_hi):
         greet(hi_peer(step), me_v)
     greet(partner, me_v)
@@ -71,7 +77,7 @@
         at = slice(c * CHUNK, (c + 1) * CHUNK)
         block(me_p, c)[...] = own[:, at] * wide[:, at]
 
-    pl.semaphore_wait(barrier, n_virt - 1 + n_hi)
+    pl.semaphore_wait(barrier, rounds + n_hi)
 
     def to_hi(step, c):
         mine = block(me_p, c)
@@ -85,13 +91,15 @@
             src_ref=held, dst_ref=held, send_sem=f_send.at[step, c], recv_sem=f_recv.at[step, c],
             device_id=(partner, me_v), device_id_type=MESH)
 
-    def to_virt(step):
+    def to_virt(turn):
+        bit = 2 ** turn
+        held = amps.at[pl.ds(pl.multiple_of((me_v // bit) * (bit * rows), bit * rows), bit * rows)]
         return pltpu.make_async_remote_copy(
-            src_ref=amp_hbm, dst_ref=my_amps, send_sem=a_send.at[step], recv_sem=a_recv.at[step],
-            device_id=(me_p, (me_v + step) % n_virt), device_id_type=MESH)
-
-    for step in range(1, n_virt):
-        to_virt(step).start()
+            src_ref=held, dst_ref=held, send_sem=a_send.at[turn], recv_sem=a_recv.at[turn],
+            device_id=(me_p, virt_peer(turn)), device_id_type=MESH)
+
+    keep.wait()
+    to_virt(0).start()
     for c in range(chunks):
         for step in range(1, n_hi):
             to_hi(step, c).start()
@@ -103,12 +111,6 @@
     tall = jnp.dot(spread(row_tiles, all_rows, 0), amp_mask[...].astype(F32).astype(BF16),
                    preferred_element_type=F32).astype(BF16)
     masked[...] = jnp.dot(tall, spread(col_tiles, depths, 1), preferred_element_type=F32).astype(BF16)
-
-    def gather_amps():
-        keep.wait()
-        for step in range(1, n_virt):
-            to_virt(step).wait_recv()
-        masked[...] = amps[...] * masked[...]
 
     def store(c):
         return pltpu.make_async_copy(result.at[c], out.at[:, pl.ds(c * CHUNK, CHUNK)], out_sem.at[c])
@@ -132,26 +134,41 @@
             lax.fori_loop(0, all_rows // part, body, 0)
         store(c).start()
 
-    late = chunks // 2
-    for c in range(chunks):
+    late = max(chunks // 2, rounds - 1)
+    for c in range(chunks):
+        if c + 1 < rounds:
+            to_virt(c).wait_recv()
+            to_virt(c + 1).start()
         for step in range(1, n_hi):
             to_hi(step, c).wait_recv()
             to_partner(step, c).start()
         if c == late:
-            gather_amps()
+            to_virt(rounds - 1).wait_recv()
+            masked[...] = amps[...] * masked[...]
         if c >= late:
             for ready in range(0 if c == late else c - 1, c):
                 multiply(ready)
     multiply(chunks - 1)
 
-    for step in range(1, n_virt):
-        to_virt(step).wait_send()
+    for turn in range(rounds):
+        to_virt(turn).wait_send()
     for c in range(chunks):
         for step in range(1, n_hi):
             to_hi(step, c).wait_send()
         for step in range(n_hi):
             to_partner(step, c).wait_send()
         store(c).wait()
+
+
+def hand_over(held, out, sem):
+    parts = sem.shape[0]
+    size = held.shape[0] // parts
+    copies = [pltpu.make_async_copy(held.at[pl.ds(i * size, size)], out.at[pl.ds(i * size, size)], sem.at[i])
+              for i in range(parts)]
+    for copy in copies:
+        copy.start()
+    for copy in copies:
+        copy.wait()
 
 
 def solution(mesh):
@@ -164,7 +181,7 @@
         chunks = columns // CHUNK
         dma = pltpu.SemaphoreType.DMA
         hbm = pl.BlockSpec(memory_space=pltpu.HBM)
-        return pl.pallas_call(
+        held = pl.pallas_call(
             functools.partial(kernel, n_pair, n_virt),
             out_shape=jax.ShapeDtypeStruct((rows * n_virt, columns), BF16),
             in_specs=[hbm] * 4,
@@ -186,6 +203,14 @@
             compiler_params=pltpu.CompilerParams(
                 collective_id=0, has_side_effects=True, vmem_limit_bytes=60 * 2 ** 20),
         )(amplitudes, integrals, amp_mask, integral_mask)
+        return pl.pallas_call(
+            hand_over,
+            out_shape=jax.ShapeDtypeStruct(held.shape, held.dtype),
+            in_specs=[hbm],
+            out_specs=hbm,
+            scratch_shapes=[dma((8,))],
+            compiler_params=pltpu.CompilerParams(vmem_limit_bytes=60 * 2 ** 20),
+        )(held)
 
     in_specs = (P(("pair", "virt"), None), P("pair", "virt"), P("pair", None), P("pair", "virt"))
     return jax.shard_map(

time: 19.7 us -> 52.9 us (2.69)
  Pallas kernels: 17.2 us -> 52.8 us
  local copies, waits for them, and re-layouts: 2.3 us -> 0 us
    pallas_call x0 -> x1, Pallas kernels: none -> 32.9 us  [on_device(): pl.pallas_call(hand_over, out_shape=jax.ShapeDtypeStruct(held.shape, held...]
    pallas_call x1, Pallas kernels: 17.2 us -> 19.8 us  [on_device(): pl.pallas_call(functools.partial(kernel, n_pair, n_virt), out_shape=jax.S...]
    unnamed x1 -> x0, local copies, waits for them, and re-layouts: 2.3 us -> none
where the time goes in v3:
time: 52.9 us; the launch traced here: 52.8 us
  Pallas kernels  52.8 us (100%)
    pallas_call x1, Pallas kernels, on_device(): pl.pallas_call(hand_over, out_shape=jax.ShapeDtypeStruct(held.shape, held...  32.9 us
    pallas_call x1, Pallas kernels, on_device(): pl.pallas_call(functools.partial(kernel, n_pair, n_virt), out_shape=jax.S...  19.8 us

profile of v3, /device:TPU:0, one launch (start us, length us, event | category | flops | bytes accessed | tf_op | source)
XLA Modules:
  0.0 52.8 jit_solution(1794525994072577994)
XLA Ops:
  0.0 19.8 %shard_map.46.held = bf16[256,2048]{1,0:T(8,128)(2,1)} custom-call(bf16[32,256]{1,0:T(8,128)(2,1)} %amp_hbm.1, bf16[64,2048]{1,0:T(8,128)(2,1)} %int_hbm.1, s32[4,4]{1,0:T(4,128)} %amp_mask_hbm.1, s32[1,32]{1,0:T(1,128)} %int_mask_hbm.1), custom_call_target="tpu_custom_call" | custom-call | tf_op jit(solution)/shard_map/pallas_call | solution.py:184
  19.9 32.9 %shard_map.47 = bf16[256,2048]{1,0:T(8,128)(2,1)} custom-call(bf16[256,2048]{1,0:T(8,128)(2,1)} %shard_map.46.held), custom_call_target="tpu_custom_call" | custom-call | tf_op jit(solution)/shard_map/pallas_call | solution.py:206

commit v4 on v1

v4 whole, which is shorter than its diff:
```python
import functools

import jax
import jax.numpy as jnp
from jax import lax
from jax.experimental import pallas as pl
from jax.experimental.pallas import tpu as pltpu
from jax.sharding import PartitionSpec as P

MESH = pl.DeviceIdType.MESH
CHUNK = 512
CORES = 2
F32 = jnp.float32
BF16 = jnp.bfloat16


def spread(tiles, length, axis):
    shape = (length, tiles) if axis == 0 else (tiles, length)
    place = lax.broadcasted_iota(jnp.int32, shape, axis)
    tile = lax.broadcasted_iota(jnp.int32, shape, 1 - axis)
    size = length // tiles
    inside = (place >= tile * size) & (place < (tile + 1) * size)
    return jnp.where(inside, 1.0, 0.0).astype(BF16)


def gather(n_pair, n_virt, amp_hbm, int_hbm, int_mask_hbm, panel, amps,
           own, own_amp, masked, landed, int_mask, load_sem, keep_sem, x_send, x_recv, x_keep,
           f_send, f_recv, a_send, a_recv):
    me_p, me_v = lax.axis_index("pair"), lax.axis_index("virt")
    n_hi = n_pair // CORES
    hi, core = me_p // CORES, me_p % CORES
    partner = hi * CORES + (1 - core)
    depth, columns = int_hbm.shape
    rows = amp_hbm.shape[0]
    chunks = panel.shape[0]

    loads = [pltpu.make_async_copy(src, dst, load_sem.at[i])
             for i, (src, dst) in enumerate(((int_mask_hbm, int_mask), (int_hbm, own), (amp_hbm, own_amp)))]
    for load in loads:
        load.start()
    barrier = pltpu.get_barrier_semaphore()

    def hi_peer(step):
        return ((hi + step) % n_hi) * CORES + core

    def greet(pair, virt):
        pl.semaphore_signal(barrier, inc=1, device_id=(pair, virt), device_id_type=MESH)

    for step in range(1, n_virt):
        greet(me_p, (me_v + step) % n_virt)
    for step in range(1, n_hi):
        greet(hi_peer(step), me_v)
    greet(partner, me_v)

    tiles = int_mask.shape[1]
    repeat = spread(tiles, columns, 1)
    loads[0].wait()
    mask = jnp.broadcast_to(int_mask[...].astype(F32), (8, tiles)).astype(BF16)
    wide = jnp.dot(mask, repeat, preferred_element_type=F32)[:1].astype(BF16)
    loads[1].wait()
    for c in range(chunks):
        at = slice(c * CHUNK, (c + 1) * CHUNK)
        masked[c] = own[:, at] * wide[:, at]
    loads[2].wait()

    pl.semaphore_wait(barrier, n_virt - 1 + n_hi)

    def rows_of(pair):
        return pl.ds(pl.multiple_of(pair * depth, depth), depth)

    my_amps = amps.at[pl.ds(pl.multiple_of(me_v * rows, rows), rows)]
    my_panel = panel.at[:, rows_of(me_p)]

    def to_hi(step, c):
        return pltpu.make_async_remote_copy(
            src_ref=masked.at[c], dst_ref=landed.at[step - 1, c],
            send_sem=x_send.at[step, c], recv_sem=x_recv.at[step, c],
            device_id=(hi_peer(step), me_v), device_id_type=MESH)

    def pass_on(step, c):
        held, place = landed.at[step - 1, c], panel.at[c, rows_of(((hi - step + n_hi) % n_hi) * CORES + core)]
        return pltpu.make_async_remote_copy(
            src_ref=held, dst_ref=place, send_sem=f_send.at[step, c], recv_sem=f_recv.at[step, c],
            device_id=(partner, me_v), device_id_type=MESH), pltpu.make_async_copy(held, place, x_keep.at[step, c])

    to_partner = pltpu.make_async_remote_copy(
        src_ref=masked, dst_ref=my_panel, send_sem=f_send.at[0, 0], recv_sem=f_recv.at[0, 0],
        device_id=(partner, me_v), device_id_type=MESH)

    def to_virt(step):
        return pltpu.make_async_remote_copy(
            src_ref=own_amp, dst_ref=my_amps, send_sem=a_send.at[step], recv_sem=a_recv.at[step],
            device_id=(me_p, (me_v + step) % n_virt), device_id_type=MESH)

    keeps = [pltpu.make_async_copy(masked, my_panel, keep_sem.at[0]),
             pltpu.make_async_copy(own_amp, my_amps, keep_sem.at[1])]
    for c in range(chunks):
        for step in range(1, n_hi):
            to_hi(step, c).start()
        if c == 0:
            for step in range(1, n_virt):
                to_virt(step).start()
    to_partner.start()
    for keep in keeps:
        keep.start()

    for c in range(chunks):
        for step in range(1, n_hi):
            to_hi(step, c).wait_recv()
            for copy in pass_on(step, c):
                copy.start()

    for keep in keeps:
        keep.wait()
    to_partner.wait()
    for step in range(1, n_virt):
        to_virt(step).wait()
    for c in range(chunks):
        for step in range(1, n_hi):
            to_hi(step, c).wait_send()
            for copy in pass_on(step, c):
                copy.wait()


def multiply(panel_hbm, amps_hbm, amp_mask_hbm, out, panel, amps, amp_mask, result, load_sem, panel_sem, out_sem):
    chunks = panel.shape[0]
    row_tiles, col_tiles = amp_mask.shape
    all_rows, depths = amps.shape
    part = min(all_rows, 256)
    loads = [pltpu.make_async_copy(amp_mask_hbm, amp_mask, load_sem.at[0]),
             pltpu.make_async_copy(amps_hbm, amps, load_sem.at[1])]
    blocks = [pltpu.make_async_copy(panel_hbm.at[c], panel.at[c], panel_sem.at[c]) for c in range(chunks)]
    stores = [pltpu.make_async_copy(result.at[c], out.at[:, pl.ds(c * CHUNK, CHUNK)], out_sem.at[c])
              for c in range(chunks)]
    for load in loads + blocks:
        load.start()
    tall, wide = spread(row_tiles, all_rows, 0), spread(col_tiles, depths, 1)
    loads[0].wait()
    tall = jnp.dot(tall, amp_mask[...].astype(F32).astype(BF16), preferred_element_type=F32).astype(BF16)
    full = jnp.dot(tall, wide, preferred_element_type=F32).astype(BF16)
    loads[1].wait()
    amps[...] = amps[...] * full

    for c in range(chunks):
        blocks[c].wait()

        def some_rows(r, carry):
            at = pl.ds(r * part, part)
            result[c, at, :] = jnp.dot(amps[at, :], panel[c], preferred_element_type=F32).astype(BF16)
            return carry

        if all_rows == part:
            some_rows(0, 0)
        else:
            lax.fori_loop(0, all_rows // part, some_rows, 0)
        stores[c].start()
    for store in stores:
        store.wait()


def solution(mesh):
    n_pair, n_virt = mesh.shape["pair"], mesh.shape["virt"]
    n_hi = n_pair // CORES

    def on_device(amplitudes, integrals, amp_mask, integral_mask):
        rows, depths = amplitudes.shape
        depth, columns = integrals.shape
        all_rows = rows * n_virt
        chunks = columns // CHUNK
        dma = pltpu.SemaphoreType.DMA
        hbm = pl.BlockSpec(memory_space=pltpu.HBM)
        whole_panel = jax.ShapeDtypeStruct((chunks, depths, CHUNK), BF16)
        whole_amps = jax.ShapeDtypeStruct((all_rows, depths), BF16)
        panel, amps = pl.pallas_call(
            functools.partial(gather, n_pair, n_virt),
            out_shape=(whole_panel, whole_amps),
            in_specs=[hbm] * 3,
            out_specs=(hbm, hbm),
            scratch_shapes=[
                pltpu.VMEM((depth, columns), BF16),
                pltpu.VMEM((rows, depths), BF16),
                pltpu.VMEM((chunks, depth, CHUNK), BF16),
                pltpu.VMEM((max(n_hi - 1, 1), chunks, depth, CHUNK), BF16),
                pltpu.VMEM(integral_mask.shape, jnp.int32),
                dma((3,)), dma((2,)),
                dma((n_hi, chunks)), dma((n_hi, chunks)), dma((n_hi, chunks)),
                dma((n_hi, chunks)), dma((n_hi, chunks)),
                dma((n_virt,)), dma((n_virt,)),
            ],
            compiler_params=pltpu.CompilerParams(
                collective_id=0, has_side_effects=True, vmem_limit_bytes=60 * 2 ** 20),
        )(amplitudes, integrals, integral_mask)
        return pl.pallas_call(
            multiply,
            out_shape=jax.ShapeDtypeStruct((all_rows, columns), BF16),
            in_specs=[hbm] * 3,
            out_specs=hbm,
            scratch_shapes=[
                pltpu.VMEM(whole_panel.shape, BF16),
                pltpu.VMEM(whole_amps.shape, BF16),
                pltpu.VMEM(amp_mask.shape, jnp.int32),
                pltpu.VMEM((chunks, all_rows, CHUNK), BF16),
                dma((2,)), dma((chunks,)), dma((chunks,)),
            ],
            compiler_params=pltpu.CompilerParams(vmem_limit_bytes=60 * 2 ** 20),
        )(panel, amps, amp_mask)

    in_specs = (P(("pair", "virt"), None), P("pair", "virt"), P("pair", None), P("pair", "virt"))
    return jax.shard_map(
        on_device, mesh=mesh, in_specs=in_specs, out_specs=P("pair", "virt"), check_vma=False
    )
```

time: 20.2 us -> 18.2 us (0.901)
  local copies, waits for them, and re-layouts: 3.97 us -> 0 us
  Pallas kernels: 15.9 us -> 18 us
    unnamed x9 -> x0, local copies, waits for them, and re-layouts: 3.97 us -> none
    pallas_call x1 -> x2, Pallas kernels: 15.9 us -> 18 us  [the longest x1 15.1 us: on_device(): pl.pallas_call(functools.partial(gather, n_pair, n_virt), out_shape=(whol...]
where the time goes in v4:
time: 18.2 us; the launch traced here: 18 us
  Pallas kernels  18 us (99%)
    pallas_call x1, Pallas kernels, on_device(): pl.pallas_call(functools.partial(gather, n_pair, n_virt), out_shape=(whol...  15.1 us
    pallas_call x1, Pallas kernels, on_device(): pl.pallas_call(multiply, out_shape=jax.ShapeDtypeStruct((all_rows, column...  2.89 us

profile of v4, /device:TPU:0, one launch (start us, length us, event | category | flops | bytes accessed | tf_op | source)
XLA Modules:
  0.0 18.0 jit_solution(4139124548671916238)
XLA Ops:
  0.0 15.1 %shard_map.46 = (bf16[4,256,512]{2,1,0:T(8,128)(2,1)}, bf16[256,256]{1,0:T(8,128)(2,1)}) custom-call(bf16[32,256]{1,0:T(8,128)(2,1)} %amp_hbm.1, bf16[64,2048]{1,0:T(8,128)(2,1)} %int_hbm.1, s32[1,32]{1,0:T(1,128)} %int_mask_hbm.1), custom_call_target="tpu_custom_call" | custom-call | tf_op jit(solution)/shard_map/pallas_call | solution.py:174
  15.1 2.9 %shard_map.47 = bf16[256,2048]{1,0:T(8,128)(2,1)} custom-call(bf16[4,256,512]{2,1,0:T(8,128)(2,1)} %get-tuple-element.7.panel_hbm, bf16[256,256]{1,0:T(8,128)(2,1)} %get-tuple-element.8.amps_hbm, s32[4,4]{1,0:T(4,128)} %amp_mask_hbm.1), custom_call_target="tpu_custom_call" | custom-call | tf_op jit(solution)/shard_map/pallas_call | solution.py:193

commit v5 on v4

v5 whole, which is shorter than its diff:
```python
import functools

import jax
import jax.numpy as jnp
from jax import lax
from jax.experimental import pallas as pl
from jax.experimental.pallas import tpu as pltpu
from jax.sharding import PartitionSpec as P

MESH = pl.DeviceIdType.MESH
CHUNK = 256
FLIGHT = 3
CORES = 2
F32 = jnp.float32
BF16 = jnp.bfloat16


def spread(tiles, length, axis):
    shape = (length, tiles) if axis == 0 else (tiles, length)
    place = lax.broadcasted_iota(jnp.int32, shape, axis)
    tile = lax.broadcasted_iota(jnp.int32, shape, 1 - axis)
    size = length // tiles
    inside = (place >= tile * size) & (place < (tile + 1) * size)
    return jnp.where(inside, 1.0, 0.0).astype(BF16)


def gather(n_pair, n_virt, amp_hbm, int_hbm, amp_mask_hbm, int_mask_hbm, panel, amps_out,
           own, amps, masked, landed, amp_mask, int_mask, load_sem, keep_sem, x_send, x_recv, x_keep,
           f_send, f_recv, y_sem, up_send, up_recv, down_send, down_recv):
    me_p, me_v = lax.axis_index("pair"), lax.axis_index("virt")
    n_hi = n_pair // CORES
    hi, core = me_p // CORES, me_p % CORES
    partner = hi * CORES + (1 - core)
    depth, columns = int_hbm.shape
    rows = amp_hbm.shape[0]
    chunks = panel.shape[0]

    line, side = me_v // 2, me_v % 2
    n_line = n_virt // 2
    beside = line * 2 + (1 - side)
    my_amps = amps.at[pl.ds(pl.multiple_of(me_v * rows, rows), rows)]
    loads = [pltpu.make_async_copy(src, dst, load_sem.at[i])
             for i, (src, dst) in enumerate(((int_mask_hbm, int_mask), (int_hbm, own), (amp_hbm, my_amps),
                                             (amp_mask_hbm, amp_mask)))]
    for load in loads:
        load.start()
    barrier = pltpu.get_barrier_semaphore()

    def hi_peer(step):
        return ((hi + step) % n_hi) * CORES + core

    def greet(pair, virt):
        pl.semaphore_signal(barrier, inc=1, device_id=(pair, virt), device_id_type=MESH)

    greet(me_p, beside)
    pl.when(line > 0)(lambda: greet(me_p, me_v - 2))
    pl.when(line < n_line - 1)(lambda: greet(me_p, me_v + 2))
    for step in range(1, n_hi):
        greet(hi_peer(step), me_v)
    greet(partner, me_v)

    tiles = int_mask.shape[1]
    repeat = spread(tiles, columns, 1)
    loads[0].wait()
    mask = jnp.broadcast_to(int_mask[...].astype(F32), (8, tiles)).astype(BF16)
    wide = jnp.dot(mask, repeat, preferred_element_type=F32)[:1].astype(BF16)
    loads[1].wait()
    for c in range(chunks):
        at = slice(c * CHUNK, (c + 1) * CHUNK)
        masked[c] = own[:, at] * wide[:, at]
    loads[2].wait()

    below, above = (line + n_line - 1) // n_line, (2 * n_line - 2 - line) // n_line
    pl.semaphore_wait(barrier, n_hi + 1 + below + above)

    def rows_of(pair):
        return pl.ds(pl.multiple_of(pair * depth, depth), depth)

    my_panel = panel.at[:, rows_of(me_p)]

    def to_hi(step, c):
        return pltpu.make_async_remote_copy(
            src_ref=masked.at[c], dst_ref=landed.at[step - 1, c],
            send_sem=x_send.at[step, c], recv_sem=x_recv.at[step, c],
            device_id=(hi_peer(step), me_v), device_id_type=MESH)

    def pass_on(step, c):
        held, place = landed.at[step - 1, c], panel.at[c, rows_of(((hi - step + n_hi) % n_hi) * CORES + core)]
        return pltpu.make_async_remote_copy(
            src_ref=held, dst_ref=place, send_sem=f_send.at[step, c], recv_sem=f_recv.at[step, c],
            device_id=(partner, me_v), device_id_type=MESH), pltpu.make_async_copy(held, place, x_keep.at[step, c])

    to_partner = pltpu.make_async_remote_copy(
        src_ref=masked, dst_ref=my_panel, send_sem=f_send.at[0, 0], recv_sem=f_recv.at[0, 0],
        device_id=(partner, me_v), device_id_type=MESH)

    to_beside = pltpu.make_async_remote_copy(
        src_ref=my_amps, dst_ref=my_amps, send_sem=y_sem.at[0], recv_sem=y_sem.at[1],
        device_id=(me_p, beside), device_id_type=MESH)

    def two(place):
        return amps.at[pl.ds(pl.multiple_of(place * (2 * rows), 2 * rows), 2 * rows)]

    def up(step):
        held = two(line - step + 1)
        return pltpu.make_async_remote_copy(
            src_ref=held, dst_ref=held, send_sem=up_send.at[step], recv_sem=up_recv.at[step],
            device_id=(me_p, me_v + 2), device_id_type=MESH)

    def down(step):
        held = two(line + step - 1)
        return pltpu.make_async_remote_copy(
            src_ref=held, dst_ref=held, send_sem=down_send.at[step], recv_sem=down_recv.at[step],
            device_id=(me_p, me_v - 2), device_id_type=MESH)

    def up_goes(step):
        return (line < n_line - 1) & (line - step + 1 >= 0)

    def down_goes(step):
        return (line > 0) & (line + step - 1 < n_line)

    def line_start(step):
        pl.when(up_goes(step))(lambda: up(step).start())
        pl.when(down_goes(step))(lambda: down(step).start())

    def line_receive(step):
        pl.when(line - step >= 0)(lambda: up(step).wait_recv())
        pl.when(line + step < n_line)(lambda: down(step).wait_recv())

    def line_sent(step):
        pl.when(up_goes(step))(lambda: up(step).wait_send())
        pl.when(down_goes(step))(lambda: down(step).wait_send())

    def start_chunk(c):
        for step in range(1, n_hi):
            to_hi(step, c).start()

    keep = pltpu.make_async_copy(masked, my_panel, keep_sem.at[0])
    to_beside.start()
    for c in range(min(FLIGHT, chunks)):
        start_chunk(c)
    to_partner.start()
    keep.start()

    row_tiles, col_tiles = amp_mask.shape
    all_rows, depths = amps.shape
    loads[3].wait()
    tall = jnp.dot(spread(row_tiles, all_rows, 0), amp_mask[...].astype(F32).astype(BF16),
                   preferred_element_type=F32).astype(BF16)
    full = jnp.dot(tall, spread(col_tiles, depths, 1), preferred_element_type=F32).astype(BF16)

    to_beside.wait_recv()
    line_start(1)
    ahead = 1
    for c in range(chunks):
        for step in range(1, n_hi):
            to_hi(step, c).wait_send()
        if c + FLIGHT < chunks:
            start_chunk(c + FLIGHT)
        for step in range(1, n_hi):
            to_hi(step, c).wait_recv()
            for copy in pass_on(step, c):
                copy.start()
        if c % 2 == 1 and ahead < n_line - 1:
            line_receive(ahead)
            ahead += 1
            line_start(ahead)

    to_beside.wait_send()
    for step in range(ahead, n_line):
        line_receive(step)
        if step + 1 < n_line:
            line_start(step + 1)
    for step in range(1, n_line):
        line_sent(step)
    amps[...] = amps[...] * full
    amps_keep = pltpu.make_async_copy(amps, amps_out, keep_sem.at[1])
    amps_keep.start()

    keep.wait()
    to_partner.wait()
    for c in range(chunks):
        for step in range(1, n_hi):
            for copy in pass_on(step, c):
                copy.wait()
    amps_keep.wait()


def multiply(panel_hbm, amps_hbm, out, panel, amps, result, load_sem, panel_sem, out_sem):
    chunks = panel.shape[0]
    all_rows = amps.shape[0]
    part = min(all_rows, 256)
    load = pltpu.make_async_copy(amps_hbm, amps, load_sem.at[0])
    blocks = [pltpu.make_async_copy(panel_hbm.at[c], panel.at[c], panel_sem.at[c]) for c in range(chunks)]
    stores = [pltpu.make_async_copy(result.at[c], out.at[:, pl.ds(c * CHUNK, CHUNK)], out_sem.at[c])
              for c in range(chunks)]
    for copy in [load] + blocks:
        copy.start()
    load.wait()

    for c in range(chunks):
        blocks[c].wait()

        def some_rows(r, carry):
            at = pl.ds(r * part, part)
            result[c, at, :] = jnp.dot(amps[at, :], panel[c], preferred_element_type=F32).astype(BF16)
            return carry

        if all_rows == part:
            some_rows(0, 0)
        else:
            lax.fori_loop(0, all_rows // part, some_rows, 0)
        stores[c].start()
    for store in stores:
        store.wait()


def solution(mesh):
    n_pair, n_virt = mesh.shape["pair"], mesh.shape["virt"]
    n_hi = n_pair // CORES

    def on_device(amplitudes, integrals, amp_mask, integral_mask):
        rows, depths = amplitudes.shape
        depth, columns = integrals.shape
        all_rows = rows * n_virt
        chunks = columns // CHUNK
        dma = pltpu.SemaphoreType.DMA
        hbm = pl.BlockSpec(memory_space=pltpu.HBM)
        whole_panel = jax.ShapeDtypeStruct((chunks, depths, CHUNK), BF16)
        whole_amps = jax.ShapeDtypeStruct((all_rows, depths), BF16)
        panel, amps = pl.pallas_call(
            functools.partial(gather, n_pair, n_virt),
            out_shape=(whole_panel, whole_amps),
            in_specs=[hbm] * 4,
            out_specs=(hbm, hbm),
            scratch_shapes=[
                pltpu.VMEM((depth, columns), BF16),
                pltpu.VMEM((all_rows, depths), BF16),
                pltpu.VMEM((chunks, depth, CHUNK), BF16),
                pltpu.VMEM((max(n_hi - 1, 1), chunks, depth, CHUNK), BF16),
                pltpu.VMEM(amp_mask.shape, jnp.int32),
                pltpu.VMEM(integral_mask.shape, jnp.int32),
                dma((4,)), dma((2,)),
                dma((n_hi, chunks)), dma((n_hi, chunks)), dma((n_hi, chunks)),
                dma((n_hi, chunks)), dma((n_hi, chunks)),
                dma((2,)),
                dma((n_virt // 2,)), dma((n_virt // 2,)), dma((n_virt // 2,)), dma((n_virt // 2,)),
            ],
            compiler_params=pltpu.CompilerParams(
                collective_id=0, has_side_effects=True, vmem_limit_bytes=60 * 2 ** 20),
        )(amplitudes, integrals, amp_mask, integral_mask)
        return pl.pallas_call(
            multiply,
            out_shape=jax.ShapeDtypeStruct((all_rows, columns), BF16),
            in_specs=[hbm] * 2,
            out_specs=hbm,
            scratch_shapes=[
                pltpu.VMEM(whole_panel.shape, BF16),
                pltpu.VMEM(whole_amps.shape, BF16),
                pltpu.VMEM((chunks, all_rows, CHUNK), BF16),
                dma((1,)), dma((chunks,)), dma((chunks,)),
            ],
            compiler_params=pltpu.CompilerParams(vmem_limit_bytes=60 * 2 ** 20),
        )(panel, amps)

    in_specs = (P(("pair", "virt"), None), P("pair", "virt"), P("pair", None), P("pair", "virt"))
    return jax.shard_map(
        on_device, mesh=mesh, in_specs=in_specs, out_specs=P("pair", "virt"), check_vma=False
    )
```

time: 18.2 us -> 22.5 us (1.24)
  Pallas kernels: 18 us -> 22.4 us
    pallas_call x1, Pallas kernels: 15.1 us -> 18.6 us  [on_device(): pl.pallas_call(functools.partial(gather, n_pair, n_virt), out_shape=(whol...]
    pallas_call x1, Pallas kernels: 2.89 us -> 3.83 us  [on_device(): pl.pallas_call(multiply, out_shape=jax.ShapeDtypeStruct((all_rows, column...]
where the time goes in v5:
time: 22.5 us; the launch traced here: 22.4 us
  Pallas kernels  22.4 us (100%)
    pallas_call x1, Pallas kernels, on_device(): pl.pallas_call(functools.partial(gather, n_pair, n_virt), out_shape=(whol...  18.6 us
    pallas_call x1, Pallas kernels, on_device(): pl.pallas_call(multiply, out_shape=jax.ShapeDtypeStruct((all_rows, column...  3.83 us

profile of v5, /device:TPU:0, one launch (start us, length us, event | category | flops | bytes accessed | tf_op | source)
XLA Modules:
  0.0 22.4 jit_solution(6991859841021108302)
XLA Ops:
  0.0 18.6 %shard_map.46 = (bf16[8,256,256]{2,1,0:T(8,128)(2,1)}, bf16[256,256]{1,0:T(8,128)(2,1)}) custom-call(bf16[32,256]{1,0:T(8,128)(2,1)} %amp_hbm.1, bf16[64,2048]{1,0:T(8,128)(2,1)} %int_hbm.1, s32[4,4]{1,0:T(4,128)} %amp_mask_hbm.1, s32[1,32]{1,0:T(1,128)} %int_mask_hbm.1), custom_call_target="tpu_custom_call" | custom-call | tf_op jit(solution)/shard_map/pallas_call | solution.py:231
  18.6 3.8 %shard_map.47 = bf16[256,2048]{1,0:T(8,128)(2,1)} custom-call(bf16[8,256,256]{2,1,0:T(8,128)(2,1)} %get-tuple-element.7.panel_hbm, bf16[256,256]{1,0:T(8,128)(2,1)} %get-tuple-element.8.amps_hbm), custom_call_target="tpu_custom_call" | custom-call | tf_op jit(solution)/shard_map/pallas_call | solution.py:252

commit v6 on v4

--- a/solution.py
+++ b/solution.py
@@ -8,7 +8,7 @@
 from jax.sharding import PartitionSpec as P
 
 MESH = pl.DeviceIdType.MESH
-CHUNK = 512
+CHUNK = 1024
 CORES = 2
 F32 = jnp.float32
 BF16 = jnp.bfloat16
@@ -23,8 +23,8 @@
     return jnp.where(inside, 1.0, 0.0).astype(BF16)
 
 
-def gather(n_pair, n_virt, amp_hbm, int_hbm, int_mask_hbm, panel, amps,
-           own, own_amp, masked, landed, int_mask, load_sem, keep_sem, x_send, x_recv, x_keep,
+def gather(n_pair, n_virt, amp_hbm, int_hbm, amp_mask_hbm, int_mask_hbm, panel, amps_out,
+           own, amps, masked, landed, amp_mask, int_mask, load_sem, keep_sem, x_send, x_recv, x_keep,
            f_send, f_recv, a_send, a_recv):
     me_p, me_v = lax.axis_index("pair"), lax.axis_index("virt")
     n_hi = n_pair // CORES
@@ -34,8 +34,10 @@
     rows = amp_hbm.shape[0]
     chunks = panel.shape[0]
 
+    my_amps = amps.at[pl.ds(pl.multiple_of(me_v * rows, rows), rows)]
     loads = [pltpu.make_async_copy(src, dst, load_sem.at[i])
-             for i, (src, dst) in enumerate(((int_mask_hbm, int_mask), (int_hbm, own), (amp_hbm, own_amp)))]
+             for i, (src, dst) in enumerate(((int_mask_hbm, int_mask), (int_hbm, own), (amp_hbm, my_amps),
+                                             (amp_mask_hbm, amp_mask)))]
     for load in loads:
         load.start()
     barrier = pltpu.get_barrier_semaphore()
@@ -68,7 +70,6 @@
     def rows_of(pair):
         return pl.ds(pl.multiple_of(pair * depth, depth), depth)
 
-    my_amps = amps.at[pl.ds(pl.multiple_of(me_v * rows, rows), rows)]
     my_panel = panel.at[:, rows_of(me_p)]
 
     def to_hi(step, c):
@@ -89,11 +90,11 @@
 
     def to_virt(step):
         return pltpu.make_async_remote_copy(
-            src_ref=own_amp, dst_ref=my_amps, send_sem=a_send.at[step], recv_sem=a_recv.at[step],
+            src_ref=my_amps, dst_ref=my_amps, send_sem=a_send.at[step], recv_sem=a_recv.at[step],
             device_id=(me_p, (me_v + step) % n_virt), device_id_type=MESH)
 
-    keeps = [pltpu.make_async_copy(masked, my_panel, keep_sem.at[0]),
-             pltpu.make_async_copy(own_amp, my_amps, keep_sem.at[1])]
+    keep = pltpu.make_async_copy(masked, my_panel, keep_sem.at[0])
+    amps_keep = pltpu.make_async_copy(amps, amps_out, keep_sem.at[1])
     for c in range(chunks):
         for step in range(1, n_hi):
             to_hi(step, c).start()
@@ -101,20 +102,29 @@
             for step in range(1, n_virt):
                 to_virt(step).start()
     to_partner.start()
-    for keep in keeps:
-        keep.start()
-
-    for c in range(chunks):
+    keep.start()
+
+    row_tiles, col_tiles = amp_mask.shape
+    all_rows, depths = amps.shape
+    loads[3].wait()
+    tall = jnp.dot(spread(row_tiles, all_rows, 0), amp_mask[...].astype(F32).astype(BF16),
+                   preferred_element_type=F32).astype(BF16)
+    full = jnp.dot(tall, spread(col_tiles, depths, 1), preferred_element_type=F32).astype(BF16)
+
+    for c in range(chunks):
+        if c == chunks - 1:
+            for step in range(1, n_virt):
+                to_virt(step).wait()
+            amps[...] = amps[...] * full
+            amps_keep.start()
         for step in range(1, n_hi):
             to_hi(step, c).wait_recv()
             for copy in pass_on(step, c):
                 copy.start()
 
-    for keep in keeps:
-        keep.wait()
+    keep.wait()
     to_partner.wait()
-    for step in range(1, n_virt):
-        to_virt(step).wait()
+    amps_keep.wait()
     for c in range(chunks):
         for step in range(1, n_hi):
             to_hi(step, c).wait_send()
@@ -122,24 +132,17 @@
                 copy.wait()
 
 
-def multiply(panel_hbm, amps_hbm, amp_mask_hbm, out, panel, amps, amp_mask, result, load_sem, panel_sem, out_sem):
+def multiply(panel_hbm, amps_hbm, out, panel, amps, result, load_sem, panel_sem, out_sem):
     chunks = panel.shape[0]
-    row_tiles, col_tiles = amp_mask.shape
-    all_rows, depths = amps.shape
+    all_rows = amps.shape[0]
     part = min(all_rows, 256)
-    loads = [pltpu.make_async_copy(amp_mask_hbm, amp_mask, load_sem.at[0]),
-             pltpu.make_async_copy(amps_hbm, amps, load_sem.at[1])]
+    load = pltpu.make_async_copy(amps_hbm, amps, load_sem.at[0])
     blocks = [pltpu.make_async_copy(panel_hbm.at[c], panel.at[c], panel_sem.at[c]) for c in range(chunks)]
     stores = [pltpu.make_async_copy(result.at[c], out.at[:, pl.ds(c * CHUNK, CHUNK)], out_sem.at[c])
               for c in range(chunks)]
-    for load in loads + blocks:
-        load.start()
-    tall, wide = spread(row_tiles, all_rows, 0), spread(col_tiles, depths, 1)
-    loads[0].wait()
-    tall = jnp.dot(tall, amp_mask[...].astype(F32).astype(BF16), preferred_element_type=F32).astype(BF16)
-    full = jnp.dot(tall, wide, preferred_element_type=F32).astype(BF16)
-    loads[1].wait()
-    amps[...] = amps[...] * full
+    for copy in [load] + blocks:
+        copy.start()
+    load.wait()
 
     for c in range(chunks):
         blocks[c].wait()
@@ -174,36 +177,36 @@
         panel, amps = pl.pallas_call(
             functools.partial(gather, n_pair, n_virt),
             out_shape=(whole_panel, whole_amps),
-            in_specs=[hbm] * 3,
+            in_specs=[hbm] * 4,
             out_specs=(hbm, hbm),
             scratch_shapes=[
                 pltpu.VMEM((depth, columns), BF16),
-                pltpu.VMEM((rows, depths), BF16),
+                pltpu.VMEM((all_rows, depths), BF16),
                 pltpu.VMEM((chunks, depth, CHUNK), BF16),
                 pltpu.VMEM((max(n_hi - 1, 1), chunks, depth, CHUNK), BF16),
+                pltpu.VMEM(amp_mask.shape, jnp.int32),
                 pltpu.VMEM(integral_mask.shape, jnp.int32),
-                dma((3,)), dma((2,)),
+                dma((4,)), dma((2,)),
                 dma((n_hi, chunks)), dma((n_hi, chunks)), dma((n_hi, chunks)),
                 dma((n_hi, chunks)), dma((n_hi, chunks)),
                 dma((n_virt,)), dma((n_virt,)),
             ],
             compiler_params=pltpu.CompilerParams(
                 collective_id=0, has_side_effects=True, vmem_limit_bytes=60 * 2 ** 20),
-        )(amplitudes, integrals, integral_mask)
+        )(amplitudes, integrals, amp_mask, integral_mask)
         return pl.pallas_call(
             multiply,
             out_shape=jax.ShapeDtypeStruct((all_rows, columns), BF16),
-            in_specs=[hbm] * 3,
+            in_specs=[hbm] * 2,
             out_specs=hbm,
             scratch_shapes=[
                 pltpu.VMEM(whole_panel.shape, BF16),
                 pltpu.VMEM(whole_amps.shape, BF16),
-                pltpu.VMEM(amp_mask.shape, jnp.int32),
                 pltpu.VMEM((chunks, all_rows, CHUNK), BF16),
-                dma((2,)), dma((chunks,)), dma((chunks,)),
+                dma((1,)), dma((chunks,)), dma((chunks,)),
             ],
             compiler_params=pltpu.CompilerParams(vmem_limit_bytes=60 * 2 ** 20),
-        )(panel, amps, amp_mask)
+        )(panel, amps)
 
     in_specs = (P(("pair", "virt"), None), P("pair", "virt"), P("pair", None), P("pair", "virt"))
     return jax.shard_map(

time: 18.2 us -> 17.7 us (0.973)
  Pallas kernels: 18 us -> 17.5 us
    pallas_call x1, Pallas kernels: 2.89 us -> 2.51 us  [on_device(): pl.pallas_call(multiply, out_shape=jax.ShapeDtypeStruct((all_rows, column...]
where the time goes in v6:
time: 17.7 us; the launch traced here: 17.5 us
  Pallas kernels  17.5 us (99%)
    pallas_call x1, Pallas kernels, on_device(): pl.pallas_call(functools.partial(gather, n_pair, n_virt), out_shape=(whol...  15 us
    pallas_call x1, Pallas kernels, on_device(): pl.pallas_call(multiply, out_shape=jax.ShapeDtypeStruct((all_rows, column...  2.51 us

profile of v6, /device:TPU:0, one launch (start us, length us, event | category | flops | bytes accessed | tf_op | source)
XLA Modules:
  0.0 17.5 jit_solution(13816062283557248897)
XLA Ops:
  0.0 15.0 %shard_map.46 = (bf16[2,256,1024]{2,1,0:T(8,128)(2,1)}, bf16[256,256]{1,0:T(8,128)(2,1)}) custom-call(bf16[32,256]{1,0:T(8,128)(2,1)} %amp_hbm.1, bf16[64,2048]{1,0:T(8,128)(2,1)} %int_hbm.1, s32[4,4]{1,0:T(4,128)} %amp_mask_hbm.1, s32[1,32]{1,0:T(1,128)} %int_mask_hbm.1), custom_call_target="tpu_custom_call" | custom-call | tf_op jit(solution)/shard_map/pallas_call | solution.py:177
  15.0 2.5 %shard_map.47 = bf16[256,2048]{1,0:T(8,128)(2,1)} custom-call(bf16[2,256,1024]{2,1,0:T(8,128)(2,1)} %get-tuple-element.7.panel_hbm, bf16[256,256]{1,0:T(8,128)(2,1)} %get-tuple-element.8.amps_hbm), custom_call_target="tpu_custom_call" | custom-call | tf_op jit(solution)/shard_map/pallas_call | solution.py:197

commit v7 on v6

--- a/solution.py
+++ b/solution.py
@@ -95,13 +95,19 @@
 
     keep = pltpu.make_async_copy(masked, my_panel, keep_sem.at[0])
     amps_keep = pltpu.make_async_copy(amps, amps_out, keep_sem.at[1])
-    for c in range(chunks):
-        for step in range(1, n_hi):
-            to_hi(step, c).start()
-        if c == 0:
-            for step in range(1, n_virt):
-                to_virt(step).start()
-    to_partner.start()
+    def send_far():
+        for c in range(chunks):
+            for step in range(1, n_hi):
+                to_hi(step, c).start()
+
+    def send_rest():
+        for step in range(1, n_virt):
+            to_virt(step).start()
+        to_partner.start()
+
+    pl.when(core == 0)(send_far)
+    send_rest()
+    pl.when(core != 0)(send_far)
     keep.start()
 
     row_tiles, col_tiles = amp_mask.shape

time: 17.7 us -> 17.7 us (level)
  no operation moved by 1% of the time
where the time goes in v7:
time: 17.7 us; the launch traced here: 17.5 us
  Pallas kernels  17.5 us (99%)
    pallas_call x1, Pallas kernels, on_device(): pl.pallas_call(functools.partial(gather, n_pair, n_virt), out_shape=(whol...  15 us
    pallas_call x1, Pallas kernels, on_device(): pl.pallas_call(multiply, out_shape=jax.ShapeDtypeStruct((all_rows, column...  2.51 us

profile of v7, /device:TPU:0, one launch (start us, length us, event | category | flops | bytes accessed | tf_op | source)
XLA Modules:
  0.0 17.5 jit_solution(9266156528767783813)
XLA Ops:
  0.0 15.0 %shard_map.46 = (bf16[2,256,1024]{2,1,0:T(8,128)(2,1)}, bf16[256,256]{1,0:T(8,128)(2,1)}) custom-call(bf16[32,256]{1,0:T(8,128)(2,1)} %amp_hbm.1, bf16[64,2048]{1,0:T(8,128)(2,1)} %int_hbm.1, s32[4,4]{1,0:T(4,128)} %amp_mask_hbm.1, s32[1,32]{1,0:T(1,128)} %int_mask_hbm.1), custom_call_target="tpu_custom_call" | custom-call | tf_op jit(solution)/shard_map/pallas_call | solution.py:183
  15.0 2.5 %shard_map.47 = bf16[256,2048]{1,0:T(8,128)(2,1)} custom-call(bf16[2,256,1024]{2,1,0:T(8,128)(2,1)} %get-tuple-element.7.panel_hbm, bf16[256,256]{1,0:T(8,128)(2,1)} %get-tuple-element.8.amps_hbm), custom_call_target="tpu_custom_call" | custom-call | tf_op jit(solution)/shard_map/pallas_call | solution.py:203

commit v8 on v6

--- a/solution.py
+++ b/solution.py
@@ -25,7 +25,7 @@
 
 def gather(n_pair, n_virt, amp_hbm, int_hbm, amp_mask_hbm, int_mask_hbm, panel, amps_out,
            own, amps, masked, landed, amp_mask, int_mask, load_sem, keep_sem, x_send, x_recv, x_keep,
-           f_send, f_recv, a_send, a_recv):
+           f_send, f_recv, a_send, a_recv, up_token, down_token):
     me_p, me_v = lax.axis_index("pair"), lax.axis_index("virt")
     n_hi = n_pair // CORES
     hi, core = me_p // CORES, me_p % CORES
@@ -34,6 +34,8 @@
     rows = amp_hbm.shape[0]
     chunks = panel.shape[0]
 
+    line, side = me_v // 2, me_v % 2
+    n_line = n_virt // 2
     my_amps = amps.at[pl.ds(pl.multiple_of(me_v * rows, rows), rows)]
     loads = [pltpu.make_async_copy(src, dst, load_sem.at[i])
              for i, (src, dst) in enumerate(((int_mask_hbm, int_mask), (int_hbm, own), (amp_hbm, my_amps),
@@ -48,8 +50,9 @@
     def greet(pair, virt):
         pl.semaphore_signal(barrier, inc=1, device_id=(pair, virt), device_id_type=MESH)
 
-    for step in range(1, n_virt):
-        greet(me_p, (me_v + step) % n_virt)
+    greet(me_p, line * 2 + (1 - side))
+    pl.when(line > 0)(lambda: greet(me_p, me_v - 2))
+    pl.when(line < n_line - 1)(lambda: greet(me_p, me_v + 2))
     for step in range(1, n_hi):
         greet(hi_peer(step), me_v)
     greet(partner, me_v)
@@ -65,7 +68,8 @@
         masked[c] = own[:, at] * wide[:, at]
     loads[2].wait()
 
-    pl.semaphore_wait(barrier, n_virt - 1 + n_hi)
+    below, above = (line + n_line - 1) // n_line, (2 * n_line - 2 - line) // n_line
+    pl.semaphore_wait(barrier, n_hi + 1 + below + above)
 
     def rows_of(pair):
         return pl.ds(pl.multiple_of(pair * depth, depth), depth)
@@ -89,20 +93,53 @@
         device_id=(partner, me_v), device_id_type=MESH)
 
     def to_virt(step):
+        other_side = side if step < n_line else 1 - side
+        peer = ((line + step % n_line) % n_line) * 2 + other_side
         return pltpu.make_async_remote_copy(
             src_ref=my_amps, dst_ref=my_amps, send_sem=a_send.at[step], recv_sem=a_recv.at[step],
-            device_id=(me_p, (me_v + step) % n_virt), device_id_type=MESH)
+            device_id=(me_p, peer), device_id_type=MESH)
+
+    def tell(token, step, virt):
+        pl.semaphore_signal(token.at[step], inc=1, device_id=(me_p, virt), device_id_type=MESH)
+
+    def tell_up(step):
+        tell(up_token, step, me_v + 2)
+
+    def tell_down(step):
+        tell(down_token, step, me_v - 2)
+
+    def reach(step):
+        def below_side():
+            pl.semaphore_wait(up_token.at[step], 1)
+            if step + 1 < n_line:
+                pl.when(line < n_line - 1)(lambda: tell_up(step + 1))
+            to_virt(n_line - step).start()
+            to_virt(2 * n_line - step).start()
+
+        def above_side():
+            pl.semaphore_wait(down_token.at[step], 1)
+            if step + 1 < n_line:
+                pl.when(line > 0)(lambda: tell_down(step + 1))
+            to_virt(step).start()
+            to_virt(n_line + step).start()
+
+        pl.when(line - step >= 0)(below_side)
+        pl.when(line + step < n_line)(above_side)
 
     keep = pltpu.make_async_copy(masked, my_panel, keep_sem.at[0])
     amps_keep = pltpu.make_async_copy(amps, amps_out, keep_sem.at[1])
-    for c in range(chunks):
+    pl.when(line < n_line - 1)(lambda: tell_up(1))
+    pl.when(line > 0)(lambda: tell_down(1))
+    for step in range(1, n_hi):
+        to_hi(step, 0).start()
+    to_virt(n_line).start()
+    for c in range(1, chunks):
         for step in range(1, n_hi):
             to_hi(step, c).start()
-        if c == 0:
-            for step in range(1, n_virt):
-                to_virt(step).start()
     to_partner.start()
     keep.start()
+    for step in range(1, n_line):
+        reach(step)
 
     row_tiles, col_tiles = amp_mask.shape
     all_rows, depths = amps.shape
@@ -112,15 +149,14 @@
     full = jnp.dot(tall, spread(col_tiles, depths, 1), preferred_element_type=F32).astype(BF16)
 
     for c in range(chunks):
-        if c == chunks - 1:
-            for step in range(1, n_virt):
-                to_virt(step).wait()
-            amps[...] = amps[...] * full
-            amps_keep.start()
         for step in range(1, n_hi):
             to_hi(step, c).wait_recv()
             for copy in pass_on(step, c):
                 copy.start()
+    for step in range(1, n_virt):
+        to_virt(step).wait()
+    amps[...] = amps[...] * full
+    amps_keep.start()
 
     keep.wait()
     to_partner.wait()
@@ -190,6 +226,7 @@
                 dma((n_hi, chunks)), dma((n_hi, chunks)), dma((n_hi, chunks)),
                 dma((n_hi, chunks)), dma((n_hi, chunks)),
                 dma((n_virt,)), dma((n_virt,)),
+                pltpu.SemaphoreType.REGULAR((n_virt // 2,)), pltpu.SemaphoreType.REGULAR((n_virt // 2,)),
             ],
             compiler_params=pltpu.CompilerParams(
                 collective_id=0, has_side_effects=True, vmem_limit_bytes=60 * 2 ** 20),

time: 17.7 us -> 15.2 us (0.86)
  Pallas kernels: 17.5 us -> 15 us
    pallas_call x1, Pallas kernels: 15 us -> 12.5 us  [on_device(): pl.pallas_call(functools.partial(gather, n_pair, n_virt), out_shape=(whol...]
where the time goes in v8:
time: 15.2 us; the launch traced here: 15.1 us
  Pallas kernels  15 us (99%)
    pallas_call x1, Pallas kernels, on_device(): pl.pallas_call(functools.partial(gather, n_pair, n_virt), out_shape=(whol...  12.5 us
    pallas_call x1, Pallas kernels, on_device(): pl.pallas_call(multiply, out_shape=jax.ShapeDtypeStruct((all_rows, column...  2.51 us

profile of v8, /device:TPU:0, one launch (start us, length us, event | category | flops | bytes accessed | tf_op | source)
XLA Modules:
  0.0 15.1 jit_solution(5338749816699899891)
XLA Ops:
  0.0 12.5 %shard_map.46 = (bf16[2,256,1024]{2,1,0:T(8,128)(2,1)}, bf16[256,256]{1,0:T(8,128)(2,1)}) custom-call(bf16[32,256]{1,0:T(8,128)(2,1)} %amp_hbm.1, bf16[64,2048]{1,0:T(8,128)(2,1)} %int_hbm.1, s32[4,4]{1,0:T(4,128)} %amp_mask_hbm.1, s32[1,32]{1,0:T(1,128)} %int_mask_hbm.1), custom_call_target="tpu_custom_call" | custom-call | tf_op jit(solution)/shard_map/pallas_call | solution.py:213
  12.5 2.5 %shard_map.47 = bf16[256,2048]{1,0:T(8,128)(2,1)} custom-call(bf16[2,256,1024]{2,1,0:T(8,128)(2,1)} %get-tuple-element.7.panel_hbm, bf16[256,256]{1,0:T(8,128)(2,1)} %get-tuple-element.8.amps_hbm), custom_call_target="tpu_custom_call" | custom-call | tf_op jit(solution)/shard_map/pallas_call | solution.py:234

commit v9 on v8

--- a/solution.py
+++ b/solution.py
@@ -23,8 +23,8 @@
     return jnp.where(inside, 1.0, 0.0).astype(BF16)
 
 
-def gather(n_pair, n_virt, amp_hbm, int_hbm, amp_mask_hbm, int_mask_hbm, panel, amps_out,
-           own, amps, masked, landed, amp_mask, int_mask, load_sem, keep_sem, x_send, x_recv, x_keep,
+def gather(n_pair, n_virt, amp_hbm, int_hbm, amp_mask_hbm, int_mask_hbm, panel, amps, wide_out,
+           own, own_amp, masked, landed, amp_mask, int_mask, wide_mask, load_sem, keep_sem, x_send, x_recv, x_keep,
            f_send, f_recv, a_send, a_recv, up_token, down_token):
     me_p, me_v = lax.axis_index("pair"), lax.axis_index("virt")
     n_hi = n_pair // CORES
@@ -38,7 +38,7 @@
     n_line = n_virt // 2
     my_amps = amps.at[pl.ds(pl.multiple_of(me_v * rows, rows), rows)]
     loads = [pltpu.make_async_copy(src, dst, load_sem.at[i])
-             for i, (src, dst) in enumerate(((int_mask_hbm, int_mask), (int_hbm, own), (amp_hbm, my_amps),
+             for i, (src, dst) in enumerate(((int_mask_hbm, int_mask), (int_hbm, own), (amp_hbm, own_amp),
                                              (amp_mask_hbm, amp_mask)))]
     for load in loads:
         load.start()
@@ -96,7 +96,7 @@
         other_side = side if step < n_line else 1 - side
         peer = ((line + step % n_line) % n_line) * 2 + other_side
         return pltpu.make_async_remote_copy(
-            src_ref=my_amps, dst_ref=my_amps, send_sem=a_send.at[step], recv_sem=a_recv.at[step],
+            src_ref=own_amp, dst_ref=my_amps, send_sem=a_send.at[step], recv_sem=a_recv.at[step],
             device_id=(me_p, peer), device_id_type=MESH)
 
     def tell(token, step, virt):
@@ -127,7 +127,8 @@
         pl.when(line + step < n_line)(above_side)
 
     keep = pltpu.make_async_copy(masked, my_panel, keep_sem.at[0])
-    amps_keep = pltpu.make_async_copy(amps, amps_out, keep_sem.at[1])
+    amps_keep = pltpu.make_async_copy(own_amp, my_amps, keep_sem.at[1])
+    wide_keep = pltpu.make_async_copy(wide_mask, wide_out, keep_sem.at[2])
     pl.when(line < n_line - 1)(lambda: tell_up(1))
     pl.when(line > 0)(lambda: tell_down(1))
     for step in range(1, n_hi):
@@ -138,6 +139,7 @@
             to_hi(step, c).start()
     to_partner.start()
     keep.start()
+    amps_keep.start()
     for step in range(1, n_line):
         reach(step)
 
@@ -146,7 +148,8 @@
     loads[3].wait()
     tall = jnp.dot(spread(row_tiles, all_rows, 0), amp_mask[...].astype(F32).astype(BF16),
                    preferred_element_type=F32).astype(BF16)
-    full = jnp.dot(tall, spread(col_tiles, depths, 1), preferred_element_type=F32).astype(BF16)
+    wide_mask[...] = jnp.dot(tall, spread(col_tiles, depths, 1), preferred_element_type=F32).astype(BF16)
+    wide_keep.start()
 
     for c in range(chunks):
         for step in range(1, n_hi):
@@ -155,12 +158,11 @@
                 copy.start()
     for step in range(1, n_virt):
         to_virt(step).wait()
-    amps[...] = amps[...] * full
-    amps_keep.start()
 
     keep.wait()
     to_partner.wait()
     amps_keep.wait()
+    wide_keep.wait()
     for c in range(chunks):
         for step in range(1, n_hi):
             to_hi(step, c).wait_send()
@@ -168,17 +170,20 @@
                 copy.wait()
 
 
-def multiply(panel_hbm, amps_hbm, out, panel, amps, result, load_sem, panel_sem, out_sem):
+def multiply(panel_hbm, amps_hbm, wide_hbm, out, panel, amps, wide_mask, result, load_sem, panel_sem, out_sem):
     chunks = panel.shape[0]
     all_rows = amps.shape[0]
     part = min(all_rows, 256)
-    load = pltpu.make_async_copy(amps_hbm, amps, load_sem.at[0])
+    loads = [pltpu.make_async_copy(amps_hbm, amps, load_sem.at[0]),
+             pltpu.make_async_copy(wide_hbm, wide_mask, load_sem.at[1])]
     blocks = [pltpu.make_async_copy(panel_hbm.at[c], panel.at[c], panel_sem.at[c]) for c in range(chunks)]
     stores = [pltpu.make_async_copy(result.at[c], out.at[:, pl.ds(c * CHUNK, CHUNK)], out_sem.at[c])
               for c in range(chunks)]
-    for copy in [load] + blocks:
+    for copy in loads + blocks:
         copy.start()
-    load.wait()
+    for load in loads:
+        load.wait()
+    amps[...] = amps[...] * wide_mask[...]
 
     for c in range(chunks):
         blocks[c].wait()
@@ -210,19 +215,20 @@
         hbm = pl.BlockSpec(memory_space=pltpu.HBM)
         whole_panel = jax.ShapeDtypeStruct((chunks, depths, CHUNK), BF16)
         whole_amps = jax.ShapeDtypeStruct((all_rows, depths), BF16)
-        panel, amps = pl.pallas_call(
+        panel, amps, wide_mask = pl.pallas_call(
             functools.partial(gather, n_pair, n_virt),
-            out_shape=(whole_panel, whole_amps),
+            out_shape=(whole_panel, whole_amps, whole_amps),
             in_specs=[hbm] * 4,
-            out_specs=(hbm, hbm),
+            out_specs=(hbm, hbm, hbm),
             scratch_shapes=[
                 pltpu.VMEM((depth, columns), BF16),
-                pltpu.VMEM((all_rows, depths), BF16),
+                pltpu.VMEM((rows, depths), BF16),
                 pltpu.VMEM((chunks, depth, CHUNK), BF16),
                 pltpu.VMEM((max(n_hi - 1, 1), chunks, depth, CHUNK), BF16),
                 pltpu.VMEM(amp_mask.shape, jnp.int32),
                 pltpu.VMEM(integral_mask.shape, jnp.int32),
-                dma((4,)), dma((2,)),
+                pltpu.VMEM(whole_amps.shape, BF16),
+                dma((4,)), dma((3,)),
                 dma((n_hi, chunks)), dma((n_hi, chunks)), dma((n_hi, chunks)),
                 dma((n_hi, chunks)), dma((n_hi, chunks)),
                 dma((n_virt,)), dma((n_virt,)),
@@ -234,16 +240,17 @@
         return pl.pallas_call(
             multiply,
             out_shape=jax.ShapeDtypeStruct((all_rows, columns), BF16),
-            in_specs=[hbm] * 2,
+            in_specs=[hbm] * 3,
             out_specs=hbm,
             scratch_shapes=[
                 pltpu.VMEM(whole_panel.shape, BF16),
                 pltpu.VMEM(whole_amps.shape, BF16),
+                pltpu.VMEM(whole_amps.shape, BF16),
                 pltpu.VMEM((chunks, all_rows, CHUNK), BF16),
-                dma((1,)), dma((chunks,)), dma((chunks,)),
+                dma((2,)), dma((chunks,)), dma((chunks,)),
             ],
             compiler_params=pltpu.CompilerParams(vmem_limit_bytes=60 * 2 ** 20),
-        )(panel, amps)
+        )(panel, amps, wide_mask)
 
     in_specs = (P(("pair", "virt"), None), P("pair", "virt"), P("pair", None), P("pair", "virt"))
     return jax.shard_map(

time: 15.2 us -> 14.9 us (0.980)
  Pallas kernels: 15 us -> 14.7 us
    pallas_call x1, Pallas kernels: 12.5 us -> 12.1 us  [on_device(): pl.pallas_call(functools.partial(gather, n_pair, n_virt), out_shape=(whol...]
where the time goes in v9:
time: 14.9 us; the launch traced here: 14.7 us
  Pallas kernels  14.7 us (99%)
    pallas_call x1, Pallas kernels, on_device(): pl.pallas_call(functools.partial(gather, n_pair, n_virt), out_shape=(whol...  12.1 us
    pallas_call x1, Pallas kernels, on_device(): pl.pallas_call(multiply, out_shape=jax.ShapeDtypeStruct((all_rows, column...  2.6 us

profile of v9, /device:TPU:0, one launch (start us, length us, event | category | flops | bytes accessed | tf_op | source)
XLA Modules:
  0.0 14.7 jit_solution(3674455654728911423)
XLA Ops:
  0.0 12.1 %shard_map.46 = (bf16[2,256,1024]{2,1,0:T(8,128)(2,1)}, bf16[256,256]{1,0:T(8,128)(2,1)}, bf16[256,256]{1,0:T(8,128)(2,1)}) custom-call(bf16[32,256]{1,0:T(8,128)(2,1)} %amp_hbm.1, bf16[64,2048]{1,0:T(8,128)(2,1)} %int_hbm.1, s32[4,4]{1,0:T(4,128)} %amp_mask_hbm.1, s32[1,32]{1,0:T(1,128)} %int_mask_hbm.1), custom_call_target="tpu_custom_call" | custom-call | tf_op jit(solution)/shard_map/pallas_call | solution.py:218
  12.1 2.6 %shard_map.47 = bf16[256,2048]{1,0:T(8,128)(2,1)} custom-call(bf16[2,256,1024]{2,1,0:T(8,128)(2,1)} %get-tuple-element.8.panel_hbm, bf16[256,256]{1,0:T(8,128)(2,1)} %get-tuple-element.9.amps_hbm, bf16[256,256]{1,0:T(8,128)(2,1)} %get-tuple-element.10.wide_hbm), custom_call_target="tpu_custom_call" | custom-call | tf_op jit(solution)/shard_map/pallas_call | solution.py:240

commit v10 on v9

--- a/solution.py
+++ b/solution.py
@@ -40,7 +40,7 @@
     loads = [pltpu.make_async_copy(src, dst, load_sem.at[i])
              for i, (src, dst) in enumerate(((int_mask_hbm, int_mask), (int_hbm, own), (amp_hbm, own_amp),
                                              (amp_mask_hbm, amp_mask)))]
-    for load in loads:
+    for load in loads[:2]:
         load.start()
     barrier = pltpu.get_barrier_semaphore()
 
@@ -56,6 +56,8 @@
     for step in range(1, n_hi):
         greet(hi_peer(step), me_v)
     greet(partner, me_v)
+    for load in loads[2:]:
+        load.start()
 
     tiles = int_mask.shape[1]
     repeat = spread(tiles, columns, 1)
@@ -63,11 +65,12 @@
     mask = jnp.broadcast_to(int_mask[...].astype(F32), (8, tiles)).astype(BF16)
     wide = jnp.dot(mask, repeat, preferred_element_type=F32)[:1].astype(BF16)
     loads[1].wait()
-    for c in range(chunks):
+
+    def fill(c):
         at = slice(c * CHUNK, (c + 1) * CHUNK)
         masked[c] = own[:, at] * wide[:, at]
-    loads[2].wait()
-
+
+    fill(0)
     below, above = (line + n_line - 1) // n_line, (2 * n_line - 2 - line) // n_line
     pl.semaphore_wait(barrier, n_hi + 1 + below + above)
 
@@ -129,20 +132,18 @@
     keep = pltpu.make_async_copy(masked, my_panel, keep_sem.at[0])
     amps_keep = pltpu.make_async_copy(own_amp, my_amps, keep_sem.at[1])
     wide_keep = pltpu.make_async_copy(wide_mask, wide_out, keep_sem.at[2])
+    for c in range(chunks):
+        if c:
+            fill(c)
+        for step in range(1, n_hi):
+            to_hi(step, c).start()
     pl.when(line < n_line - 1)(lambda: tell_up(1))
     pl.when(line > 0)(lambda: tell_down(1))
-    for step in range(1, n_hi):
-        to_hi(step, 0).start()
+    loads[2].wait()
     to_virt(n_line).start()
-    for c in range(1, chunks):
-        for step in range(1, n_hi):
-            to_hi(step, c).start()
     to_partner.start()
     keep.start()
     amps_keep.start()
-    for step in range(1, n_line):
-        reach(step)
-
     row_tiles, col_tiles = amp_mask.shape
     all_rows, depths = amps.shape
     loads[3].wait()
@@ -150,6 +151,8 @@
                    preferred_element_type=F32).astype(BF16)
     wide_mask[...] = jnp.dot(tall, spread(col_tiles, depths, 1), preferred_element_type=F32).astype(BF16)
     wide_keep.start()
+    for step in range(1, n_line):
+        reach(step)
 
     for c in range(chunks):
         for step in range(1, n_hi):

time: 14.9 us -> 14.9 us (level)
  no operation moved by 1% of the time
where the time goes in v10:
time: 14.9 us; the launch traced here: 14.7 us
  Pallas kernels  14.7 us (99%)
    pallas_call x1, Pallas kernels, on_device(): pl.pallas_call(functools.partial(gather, n_pair, n_virt), out_shape=(whol...  12.1 us
    pallas_call x1, Pallas kernels, on_device(): pl.pallas_call(multiply, out_shape=jax.ShapeDtypeStruct((all_rows, column...  2.6 us

profile of v10, /device:TPU:0, one launch (start us, length us, event | category | flops | bytes accessed | tf_op | source)
XLA Modules:
  0.0 14.7 jit_solution(1400234885090103455)
XLA Ops:
  0.0 12.1 %shard_map.46 = (bf16[2,256,1024]{2,1,0:T(8,128)(2,1)}, bf16[256,256]{1,0:T(8,128)(2,1)}, bf16[256,256]{1,0:T(8,128)(2,1)}) custom-call(bf16[32,256]{1,0:T(8,128)(2,1)} %amp_hbm.1, bf16[64,2048]{1,0:T(8,128)(2,1)} %int_hbm.1, s32[4,4]{1,0:T(4,128)} %amp_mask_hbm.1, s32[1,32]{1,0:T(1,128)} %int_mask_hbm.1), custom_call_target="tpu_custom_call" | custom-call | tf_op jit(solution)/shard_map/pallas_call | solution.py:221
  12.1 2.6 %shard_map.47 = bf16[256,2048]{1,0:T(8,128)(2,1)} custom-call(bf16[2,256,1024]{2,1,0:T(8,128)(2,1)} %get-tuple-element.8.panel_hbm, bf16[256,256]{1,0:T(8,128)(2,1)} %get-tuple-element.9.amps_hbm, bf16[256,256]{1,0:T(8,128)(2,1)} %get-tuple-element.10.wide_hbm), custom_call_target="tpu_custom_call" | custom-call | tf_op jit(solution)/shard_map/pallas_call | solution.py:243

commit v11 on v10

--- a/solution.py
+++ b/solution.py
@@ -79,14 +79,19 @@
 
     my_panel = panel.at[:, rows_of(me_p)]
 
+    def half(c):
+        return pl.ds((c % 2) * (depth // 2), depth // 2)
+
     def to_hi(step, c):
         return pltpu.make_async_remote_copy(
-            src_ref=masked.at[c], dst_ref=landed.at[step - 1, c],
+            src_ref=masked.at[c // 2, half(c)], dst_ref=landed.at[step - 1, c // 2, half(c)],
             send_sem=x_send.at[step, c], recv_sem=x_recv.at[step, c],
             device_id=(hi_peer(step), me_v), device_id_type=MESH)
 
     def pass_on(step, c):
-        held, place = landed.at[step - 1, c], panel.at[c, rows_of(((hi - step + n_hi) % n_hi) * CORES + core)]
+        first = (((hi - step + n_hi) % n_hi) * CORES + core) * depth + (c % 2) * (depth // 2)
+        held = landed.at[step - 1, c // 2, half(c)]
+        place = panel.at[c // 2, pl.ds(pl.multiple_of(first, depth // 2), depth // 2)]
         return pltpu.make_async_remote_copy(
             src_ref=held, dst_ref=place, send_sem=f_send.at[step, c], recv_sem=f_recv.at[step, c],
             device_id=(partner, me_v), device_id_type=MESH), pltpu.make_async_copy(held, place, x_keep.at[step, c])
@@ -132,9 +137,9 @@
     keep = pltpu.make_async_copy(masked, my_panel, keep_sem.at[0])
     amps_keep = pltpu.make_async_copy(own_amp, my_amps, keep_sem.at[1])
     wide_keep = pltpu.make_async_copy(wide_mask, wide_out, keep_sem.at[2])
-    for c in range(chunks):
-        if c:
-            fill(c)
+    for c in range(2 * chunks):
+        if c and c % 2 == 0:
+            fill(c // 2)
         for step in range(1, n_hi):
             to_hi(step, c).start()
     pl.when(line < n_line - 1)(lambda: tell_up(1))
@@ -154,7 +159,7 @@
     for step in range(1, n_line):
         reach(step)
 
-    for c in range(chunks):
+    for c in range(2 * chunks):
         for step in range(1, n_hi):
             to_hi(step, c).wait_recv()
             for copy in pass_on(step, c):
@@ -166,7 +171,7 @@
     to_partner.wait()
     amps_keep.wait()
     wide_keep.wait()
-    for c in range(chunks):
+    for c in range(2 * chunks):
         for step in range(1, n_hi):
             to_hi(step, c).wait_send()
             for copy in pass_on(step, c):
@@ -232,8 +237,8 @@
                 pltpu.VMEM(integral_mask.shape, jnp.int32),
                 pltpu.VMEM(whole_amps.shape, BF16),
                 dma((4,)), dma((3,)),
-                dma((n_hi, chunks)), dma((n_hi, chunks)), dma((n_hi, chunks)),
-                dma((n_hi, chunks)), dma((n_hi, chunks)),
+                dma((n_hi, 2 * chunks)), dma((n_hi, 2 * chunks)), dma((n_hi, 2 * chunks)),
+                dma((n_hi, 2 * chunks)), dma((n_hi, 2 * chunks)),
                 dma((n_virt,)), dma((n_virt,)),
                 pltpu.SemaphoreType.REGULAR((n_virt // 2,)), pltpu.SemaphoreType.REGULAR((n_virt // 2,)),
             ],

time: 14.9 us -> 15 us (level)
  no operation moved by 1% of the time
where the time goes in v11:
time: 15 us; the launch traced here: 14.8 us
  Pallas kernels  14.8 us (99%)
    pallas_call x1, Pallas kernels, on_device(): pl.pallas_call(functools.partial(gather, n_pair, n_virt), out_shape=(whol...  12.2 us
    pallas_call x1, Pallas kernels, on_device(): pl.pallas_call(multiply, out_shape=jax.ShapeDtypeStruct((all_rows, column...  2.6 us

profile of v11, /device:TPU:0, one launch (start us, length us, event | category | flops | bytes accessed | tf_op | source)
XLA Modules:
  0.0 14.8 jit_solution(1228786002765360080)
XLA Ops:
  0.0 12.2 %shard_map.46 = (bf16[2,256,1024]{2,1,0:T(8,128)(2,1)}, bf16[256,256]{1,0:T(8,128)(2,1)}, bf16[256,256]{1,0:T(8,128)(2,1)}) custom-call(bf16[32,256]{1,0:T(8,128)(2,1)} %amp_hbm.1, bf16[64,2048]{1,0:T(8,128)(2,1)} %int_hbm.1, s32[4,4]{1,0:T(4,128)} %amp_mask_hbm.1, s32[1,32]{1,0:T(1,128)} %int_mask_hbm.1), custom_call_target="tpu_custom_call" | custom-call | tf_op jit(solution)/shard_map/pallas_call | solution.py:226
  12.2 2.6 %shard_map.47 = bf16[256,2048]{1,0:T(8,128)(2,1)} custom-call(bf16[2,256,1024]{2,1,0:T(8,128)(2,1)} %get-tuple-element.8.panel_hbm, bf16[256,256]{1,0:T(8,128)(2,1)} %get-tuple-element.9.amps_hbm, bf16[256,256]{1,0:T(8,128)(2,1)} %get-tuple-element.10.wide_hbm), custom_call_target="tpu_custom_call" | custom-call | tf_op jit(solution)/shard_map/pallas_call | solution.py:248
